TPU v7x, 256 devices: a whole 4x4x8 slice. The times are simulated.
256 devices in a mesh: image: 16 (over z_lo, x, core), space: 16 (over z_hi, y).
Axes of the slice: x: 4, y: 4, z: 8 (z_hi: 4, z_lo: 2; z = z_hi * 2 + z_lo), core: 2. Of those that a mesh axis runs over, the one named last changes fastest.
Arguments:
- magnetization: float32 [16, 3, 128, 128, 128], P('image', None, 'space'), may hold values from -1 to 1, as said below
- region_labels: int32 [128, 128, 128], P('space'), may hold values from 0 to 7
- demag_kernel: float32 [6, 128, 128, 128], P(None, None, 'space'), may hold values from -0.3 to 0.6
- anisotropy: float32 [8], replicated, may hold values from 0.2 to 2
- stiffness: float32 [8], replicated, may hold values from 0.05 to 0.5
Outputs:
- relaxed_path: float32 [16, 3, 128, 128, 128], P('image', None, 'space')
- band_force: float32 [16, 3, 128, 128, 128], P('image', None, 'space')
Inputs may be any that keep to these rules, and one draw needn't show every extreme that they name: `magnetization`: each cell's three components form a unit vector; the first and last images are the band's fixed ends.
All inputs are finite; a program needn't handle non-finite values.
Results may differ from a plain program's by a relative error of at most 0.0003.
Values sent between devices are 32-bit elements; how exact they have to be, the bound alone decides.
A program may use at most 128 MiB of HBM per device.

v0:
```python
import math

import jax
import jax.numpy as jnp
from jax import lax
from jax.sharding import PartitionSpec as P

STEP_SIZE = 0.2
SPRING = 4.0
EPSILON = 1e-06
TENSOR_ROWS = ((0, 3, 4), (3, 1, 5), (4, 5, 2))
CONTRACT_FORMS = {2: "icxyz,xk->ickyz", 3: "icxyz,yk->icxkz", 4: "icxyz,zk->icxyk"}


def padded_2(block, sides, width, periodic):
    for axis, dim in sides:
        count = lax.axis_size(axis)
        forward = [(i, i + 1) for i in range(count - 1)]
        if periodic:
            forward.append((count - 1, 0))
        backward = [(target, source) for source, target in forward]
        low = lax.ppermute(
            lax.slice_in_dim(block, block.shape[dim] - width, None, axis=dim), axis, forward
        )
        high = lax.ppermute(lax.slice_in_dim(block, 0, width, axis=dim), axis, backward)
        block = jnp.concatenate([low, block, high], axis=dim)
    return block


def dft_tables(grid_len):
    indices = jnp.arange(grid_len, dtype=jnp.int32)
    product = indices[:, None] * indices[None, :] % grid_len
    angles = product.astype(jnp.float32) * (2.0 * math.pi / grid_len)
    return (jnp.cos(angles), jnp.sin(angles))


def contract(values, matrix, axis_dim):
    return jnp.einsum(CONTRACT_FORMS[axis_dim], values, matrix, precision=lax.Precision.HIGHEST)


def turn(real_part, imag_part, axis_dim, cosine_table, sine_table, inverse):
    real_cos = contract(real_part, cosine_table, axis_dim)
    real_sin = contract(real_part, sine_table, axis_dim)
    imag_cos = contract(imag_part, cosine_table, axis_dim)
    imag_sin = contract(imag_part, sine_table, axis_dim)
    if inverse:
        return (real_cos - imag_sin, imag_cos + real_sin)
    return (real_cos + imag_sin, imag_cos - real_sin)


def region_value(region_labels, region_table):
    total = jnp.zeros(region_labels.shape, jnp.float32)
    for region in range(region_table.shape[0]):
        total = total + jnp.where(
            region_labels == region, region_table[region], jnp.zeros((), jnp.float32)
        )
    return total


def angle_parts(leading, trailing):
    cross_x = leading[:, 1] * trailing[:, 2] - leading[:, 2] * trailing[:, 1]
    cross_y = leading[:, 2] * trailing[:, 0] - leading[:, 0] * trailing[:, 2]
    cross_z = leading[:, 0] * trailing[:, 1] - leading[:, 1] * trailing[:, 0]
    sine_term = jnp.sqrt(cross_x * cross_x + cross_y * cross_y + cross_z * cross_z)
    cosine = jnp.sum(leading * trailing, axis=1)
    return jnp.sum(jnp.arctan2(sine_term, cosine) ** 2, axis=(1, 2, 3))


def kernel_apply(spec_real, spec_imag, kernel_part, cosine_table, sine_table):
    spec_real, spec_imag = turn(spec_real, spec_imag, 2, cosine_table, sine_table, False)
    out_real = []
    out_imag = []
    for kernel_row in TENSOR_ROWS:
        out_real.append(
            -(
                kernel_part[kernel_row[0]] * spec_real[:, 0]
                + kernel_part[kernel_row[1]] * spec_real[:, 1]
                + kernel_part[kernel_row[2]] * spec_real[:, 2]
            )
        )
        out_imag.append(
            -(
                kernel_part[kernel_row[0]] * spec_imag[:, 0]
                + kernel_part[kernel_row[1]] * spec_imag[:, 1]
                + kernel_part[kernel_row[2]] * spec_imag[:, 2]
            )
        )
    return turn(
        jnp.stack(out_real, axis=1), jnp.stack(out_imag, axis=1), 2, cosine_table, sine_table, True
    )


def effective_field(
    moment, demag_kernel, anis_cell, stiff_cell, cosine_table, sine_table, cell_count, easy_axis
):
    grid_len = cosine_table.shape[0]
    half_len = grid_len // 2
    padded = padded_2(moment, (("space", 2),), 1, True)
    laplace = padded[:, :, 2:] + padded[:, :, :-2] - 6.0 * moment
    for axis_dim in (3, 4):
        laplace = laplace + jnp.roll(moment, 1, axis_dim) + jnp.roll(moment, -1, axis_dim)
    bin_sets = ((0, half_len), (half_len, grid_len))
    weights = jnp.ones((grid_len,), jnp.float32)
    spectra = []
    for bounds in bin_sets:
        part_real = contract(moment, cosine_table[:, bounds[0] : bounds[1]], 4)
        part_imag = -contract(moment, sine_table[:, bounds[0] : bounds[1]], 4)
        part_real, part_imag = turn(part_real, part_imag, 3, cosine_table, sine_table, False)
        spectra.append(part_real)
        spectra.append(part_imag)
    low_real, low_imag = kernel_apply(
        lax.all_to_all(spectra[0], "space", split_axis=3, concat_axis=2, tiled=True),
        lax.all_to_all(spectra[1], "space", split_axis=3, concat_axis=2, tiled=True),
        demag_kernel[..., bin_sets[0][0] : bin_sets[0][1]],
        cosine_table,
        sine_table,
    )
    high_real, high_imag = kernel_apply(
        lax.all_to_all(spectra[2], "space", split_axis=3, concat_axis=2, tiled=True),
        lax.all_to_all(spectra[3], "space", split_axis=3, concat_axis=2, tiled=True),
        demag_kernel[..., bin_sets[1][0] : bin_sets[1][1]],
        cosine_table,
        sine_table,
    )
    returned = (
        lax.all_to_all(low_real, "space", split_axis=2, concat_axis=3, tiled=True),
        lax.all_to_all(low_imag, "space", split_axis=2, concat_axis=3, tiled=True),
        lax.all_to_all(high_real, "space", split_axis=2, concat_axis=3, tiled=True),
        lax.all_to_all(high_imag, "space", split_axis=2, concat_axis=3, tiled=True),
    )
    demag_part = jnp.zeros_like(moment)
    for set_index in range(2):
        start, stop = bin_sets[set_index]
        back_real, back_imag = turn(
            returned[2 * set_index], returned[2 * set_index + 1], 3, cosine_table, sine_table, True
        )
        weight_part = weights[start:stop][:, None]
        demag_part = (
            demag_part
            + contract(back_real, weight_part * cosine_table[start:stop, :], 4)
            - contract(back_imag, weight_part * sine_table[start:stop, :], 4)
        )
    demag_part = demag_part / cell_count
    return stiff_cell * laplace + demag_part + 2.0 * anis_cell * moment[:, 2:3] * easy_axis


def local(magnetization, region_labels, demag_kernel, anisotropy, stiffness):
    images_here = magnetization.shape[0]
    grid_len = magnetization.shape[3]
    cell_count = grid_len * grid_len * grid_len
    cosine_table, sine_table = dft_tables(grid_len)
    image_count = lax.axis_size("image") * images_here
    global_index = lax.axis_index("image") * images_here + jnp.arange(images_here, dtype=jnp.int32)
    movable = ((global_index > 0) & (global_index < image_count - 1)).astype(jnp.float32)[
        :, None, None, None, None
    ]
    anis_cell = region_value(region_labels, anisotropy)[None, None]
    stiff_cell = region_value(region_labels, stiffness)[None, None]
    easy_axis = jnp.array([0.0, 0.0, 1.0], jnp.float32)[None, :, None, None, None]
    sum_axes = (1, 2, 3, 4)
    moment = magnetization
    gradient = -effective_field(
        moment, demag_kernel, anis_cell, stiff_cell, cosine_table, sine_table, cell_count, easy_axis
    )
    g_perp = gradient - jnp.sum(gradient * moment, axis=1, keepdims=True) * moment
    extended = padded_2(moment, (("image", 0),), 1, False)
    preceding = extended[:-2]
    following = extended[2:]
    tangent = following - preceding
    tangent = tangent - jnp.sum(tangent * moment, axis=1, keepdims=True) * moment
    part_next = angle_parts(moment, following)
    part_prev = angle_parts(preceding, moment)
    tangent_sq = lax.psum(jnp.sum(tangent * tangent, axis=sum_axes), "space")
    factor = jnp.sqrt(cell_count / (tangent_sq + EPSILON))
    unit_tangent = tangent * factor[:, None, None, None, None]
    slope_unit, next_sq, prev_sq = lax.psum(
        (jnp.sum(g_perp * unit_tangent, axis=sum_axes), part_next, part_prev), "space"
    )
    along_term = slope_unit / cell_count
    spring_term = SPRING * (jnp.sqrt(next_sq / cell_count) - jnp.sqrt(prev_sq / cell_count))
    band_force = movable * (
        -g_perp + (along_term + spring_term)[:, None, None, None, None] * unit_tangent
    )
    stepped = moment + STEP_SIZE * band_force
    moment = stepped / jnp.sqrt(jnp.sum(stepped * stepped, axis=1, keepdims=True))
    return (moment, band_force)


def solution(mesh):
    in_specs = (
        P("image", None, "space", None, None),
        P("space", None, None),
        P(None, None, "space", None),
        P(),
        P(),
    )
    out_specs = (P("image", None, "space", None, None), P("image", None, "space", None, None))
    return jax.shard_map(local, mesh=mesh, in_specs=in_specs, out_specs=out_specs, check_vma=False)
```

profile of v0, /device:TPU:8, one launch (start us, length us, event | category | flops | bytes accessed | tf_op | source)
XLA Modules:
  0.0 501.7 jit_solution(149180708665227052)
XLA Ops:
  1.9 4.2 collective-permute-start.3
  6.7 3.4 fusion.42
  18.5 3.1 reshape.523
  21.6 11.6 %all-to-all-start = ((f32[16,1,12288]{2,1,0:T(1,128)}), f32[16,1,12288]{2,1,0:T(1,128)}, u32[]{:S(2)}, u32[]{:S(2)}) async-start(f32[16,1,12288]{2,1,0:T(1,128)} %reshape.523), calls=%async_computation | async-start | bytes 1572864 | tf_op jit(solution)/shard_map/all_to_all | solution.py:112
  41.1 3.5 fusion.300
  49.3 3.1 reshape.521
  73.5 3.1 reshape.515
  83.5 3.1 reshape.513
  98.9 12.7 %all-to-all-start.1 = ((f32[16,1,12288]{2,1,0:T(1,128)}), f32[16,1,12288]{2,1,0:T(1,128)}, u32[]{:S(2)}, u32[]{:S(2)}) async-start(f32[16,1,12288]{2,1,0:T(1,128)} %reshape.521), calls=%async_computation.1 | async-start | bytes 1572864 | tf_op jit(solution)/shard_map/all_to_all | solution.py:113
  112.2 7.8 %select_add_fusion = (f32[8,128,128]{2,1,0:T(8,128)}, pred[8,128,128]{2,1,0:T(8,128)(4,1)S(1)}, pred[8,128,128]{2,1,0:T(8,128)(4,1)S(1)}, pred[8,128,128]{2,1,0:...) fusion(f32[]{:T(128)} %bitcast.7, f32[]{:T(128)} %bitcast.6, ...), kind=kLoop, calls=%fused_computation.102 | loop fusion | flops 3014656 | bytes 2097184 | tf_op jit(solution)/shard_map/add | solution.py:54
  120.0 6.3 %fusion.92 = f32[8,128,128]{2,1,0:T(8,128)} fusion(pred[8,128,128]{2,1,0:T(8,128)(4,1)S(1)} %get-tuple-element.25, pred[8,128,128]{2,1,0:T(8,128)(4,1)S(1)} %get-tuple-element.24, pred[8,128,128]{2,1,0:T(8,128)(4,1)S(1)} %get-tuple-element.23, pred[8,128,128]{2,1,0:T(8,128)(4,1)S(1)} %get-tuple-element.22, pred[8,128,128]{2,1,0:T(8,128)(4,1)S(1)} %get-tuple-element.21, ...), kind=kLoop, calls=%fused_computation.101 | loop fusion | flops 2228224 | bytes 2097184 | tf_op jit(solution)/shard_map/mul | solution.py:144
  129.1 4.6 reduce.16
  133.6 2.9 reshape.524
  142.4 3.0 fusion.144
  145.4 10.2 %all-to-all-start.4 = ((f32[16,1,12288]{2,1,0:T(1,128)}), f32[16,1,12288]{2,1,0:T(1,128)}, u32[]{:S(2)}, u32[]{:S(2)}) async-start(f32[16,1,12288]{2,1,0:T(1,128)} %reshape.515), calls=%async_computation.4 | async-start | bytes 1572864 | tf_op jit(solution)/shard_map/all_to_all | solution.py:119
  155.6 4.5 reduce.15
  160.1 2.9 reshape.522
  179.2 9.9 %all-to-all-start.5 = ((f32[16,1,12288]{2,1,0:T(1,128)}), f32[16,1,12288]{2,1,0:T(1,128)}, u32[]{:S(2)}, u32[]{:S(2)}) async-start(f32[16,1,12288]{2,1,0:T(1,128)} %reshape.513), calls=%async_computation.5 | async-start | bytes 1572864 | tf_op jit(solution)/shard_map/all_to_all | solution.py:120
  195.1 3.1 reshape.527
  205.3 3.1 reshape.525
  208.5 4.6 reduce.12
  213.0 2.9 reshape.516
  221.7 3.1 fusion.131
  224.8 10.0 %all-to-all-start.2 = ((f32[16,1,12288]{2,1,0:T(1,128)}), f32[16,1,12288]{2,1,0:T(1,128)}, u32[]{:S(2)}, u32[]{:S(2)}) async-start(f32[16,1,12288]{2,1,0:T(1,128)} %reshape.527), calls=%async_computation.2 | async-start | bytes 1572864 | tf_op jit(solution)/shard_map/all_to_all | solution.py:126
  234.8 4.5 reduce.11
  239.3 2.9 reshape.514
  257.0 9.6 %all-to-all-start.3 = ((f32[16,1,12288]{2,1,0:T(1,128)}), f32[16,1,12288]{2,1,0:T(1,128)}, u32[]{:S(2)}, u32[]{:S(2)}) async-start(f32[16,1,12288]{2,1,0:T(1,128)} %reshape.525), calls=%async_computation.3 | async-start | bytes 1572864 | tf_op jit(solution)/shard_map/all_to_all | solution.py:127
  275.9 3.1 reshape.517
  279.0 6.0 %all-to-all-done.3 = f32[16,1,12288]{2,1,0:T(1,128)} async-done(((f32[16,1,12288]{2,1,0:T(1,128)}), f32[16,1,12288]{2,1,0:T(1,128)}, u32[]{:S(2)}, u32[]{:S(2)}) %all-to-all-start.3) | async-done | bytes 786464 | tf_op jit(solution)/shard_map/all_to_all | solution.py:127
  285.1 7.0 %all-to-all-start.7 = ((f32[16,1,12288]{2,1,0:T(1,128)}), f32[16,1,12288]{2,1,0:T(1,128)}, u32[]{:S(2)}, u32[]{:S(2)}) async-start(f32[16,1,12288]{2,1,0:T(1,128)} %reshape.517), calls=%async_computation.7 | async-start | bytes 1572864 | tf_op jit(solution)/shard_map/all_to_all | solution.py:129
  302.3 3.1 reshape.519
  305.4 4.5 reduce.17
  315.5 9.8 %all-to-all-start.6 = ((f32[16,1,12288]{2,1,0:T(1,128)}), f32[16,1,12288]{2,1,0:T(1,128)}, u32[]{:S(2)}, u32[]{:S(2)}) async-start(f32[16,1,12288]{2,1,0:T(1,128)} %reshape.519), calls=%async_computation.6 | async-start | bytes 1572864 | tf_op jit(solution)/shard_map/all_to_all | solution.py:128
  325.3 5.0 fusion.18
  330.2 4.6 reduce.18
  334.8 2.9 reshape.528
  340.4 4.5 reduce.13
  349.7 3.5 fusion.20
  353.3 3.8 fusion.12
  359.7 3.8 fusion.97
  363.5 3.5 fusion.10
  367.0 4.5 reduce.14
  376.5 3.1 fusion.67
  390.5 7.9 %multiply_reduce_fusion.6 = (f32[8,128,128]{2,1,0:T(8,128)}, f32[8,128,128]{2,1,0:T(8,128)S(1)}, f32[1,3,8,128,128]{4,3,2,1,0:T(8,128)S(1)}, f32[1,3,8,128,128]{4,3,2,1,0:T(8,128)}) fusion(f32[1,3,8,128,128]{4,3,2,1,0:T(8,128)S(1)} %copy-done, f32[1,3,8,128,128]{4,3,2,1,0:T(8,128)S(1)} %collective-permute-done.2, ...), kind=kOutput, calls=%fused_computation.50 | convolution fusion | flops 312344576 | bytes 22216716 | tf_op jit(solution)/shard_map/icxyz,zk->icxyk/dot_general | solution.py:38
  400.6 40.5 %psum.28 = f32[1]{0:T(128)} all-reduce(f32[1]{0:T(128)} %bitcast.192), channel_id=1, replica_groups=mesh['image'=16,'space'=16] {'space'}, use_global_device_ids=true, to_apply=%region_3.4 | all-reduce | flops 1 | bytes 8 | tf_op jit(solution)/shard_map/psum | solution.py:173
  441.8 3.9 multiply_reduce_fusion.1
  445.7 4.4 fusion.89
  450.0 45.1 %all-reduce = (f32[1]{0:T(128)}, f32[1]{0:T(128)}, f32[1]{0:T(128)}) all-reduce(f32[1]{0:T(128)} %bitcast.194, f32[1]{0:T(128)} %bitcast.196, f32[1]{0:T(128)} %bitcast.198), channel_id=1, replica_groups=mesh['image'=16,'space'=16] {'space'}, use_global_device_ids=true, to_apply=%region_5.6 | all-reduce | flops 3 | bytes 24 | tf_op jit(solution)/shard_map/psum | solution.py:176
  (227 shorter events, 179.3 us)
Async XLA Ops:
  0.6 389.8 %collective-permute-start.2 = (f32[1,3,8,128,128]{4,3,2,1,0:T(8,128)}, f32[1,3,8,128,128]{4,3,2,1,0:T(8,128)S(1)}, u32[]{:S(2)}, u32[]{:S(2)}) collective-permute-start(f32[1,3,8,128,128]{4,3,2,1,0:T(8,128)} %param.6), channel_id=1, source_target_pairs={{16,0},{32,16},{48,32},{64,48},{80,64},{96,80},{112,96},{128,112},... | collective-permute-start | bytes 4718600 | tf_op jit(solution)/shard_map/ppermute | solution.py:25
  1.9 388.5 %collective-permute-start.3 = (f32[1,3,8,128,128]{4,3,2,1,0:T(8,128)}, f32[1,3,8,128,128]{4,3,2,1,0:T(8,128)}, u32[]{:S(2)}, u32[]{:S(2)}) collective-permute-start(f32[1,3,8,128,128]{4,3,2,1,0:T(8,128)} %param.6), channel_id=1, source_target_pairs={{0,16},{16,32},{32,48},{48,64},{64,80},{80,96},{96,112},{112,128},... | collective-permute-start | bytes 4718600 | tf_op jit(solution)/shard_map/ppermute | solution.py:22
  6.7 4.4 copy-start
  10.1 2.9 copy-start.16
  21.6 77.4 %all-to-all-start = ((f32[16,1,12288]{2,1,0:T(1,128)}), f32[16,1,12288]{2,1,0:T(1,128)}, u32[]{:S(2)}, u32[]{:S(2)}) async-start(f32[16,1,12288]{2,1,0:T(1,128)} %reshape.523), calls=%async_computation | async-start | bytes 1572864 | tf_op jit(solution)/shard_map/all_to_all | solution.py:112
  33.9 356.5 %collective-permute-start = (f32[1,3,1,128,128]{4,3,2,1,0:T(8,128)}, f32[1,3,1,128,128]{4,3,2,1,0:T(8,128)}, u32[]{:S(2)}, u32[]{:S(2)}) collective-permute-start(f32[1,3,1,128,128]{4,3,2,1,0:T(8,128)} %get-tuple-element.46), channel_id=1, source_target_pairs={{1,0},{2,1},{3,2},{4,3},{5,4},{6,5},{7,6},{8,7},{9,8},{10,9},{11,1... | collective-permute-start | bytes 589832 | tf_op jit(solution)/shard_map/ppermute | solution.py:25
  34.0 356.3 %collective-permute-start.1 = (f32[1,3,1,128,128]{4,3,2,1,0:T(8,128)}, f32[1,3,1,128,128]{4,3,2,1,0:T(8,128)}, u32[]{:S(2)}, u32[]{:S(2)}) collective-permute-start(f32[1,3,1,128,128]{4,3,2,1,0:T(8,128)} %get-tuple-element.47), channel_id=1, source_target_pairs={{0,1},{1,2},{2,3},{3,4},{4,5},{5,6},{6,7},{7,8},{8,9},{9,10},{10,1... | collective-permute-start | bytes 589832 | tf_op jit(solution)/shard_map/ppermute | solution.py:22
  36.1 5.0 %copy-start.4 = (f32[6,128,8,128]{3,2,1,0:T(8,128)S(1)}, f32[6,128,8,128]{3,2,1,0:T(8,128)}, u32[]{:S(2)}) copy-start(f32[6,128,8,128]{3,2,1,0:T(8,128)} %param.8) | copy-start | bytes 9437188
  41.1 3.5 copy-start.17
  76.6 2.2 copy-start.15
  89.8 7.7 %copy-start.54 = (f32[8]{0:T(128)S(1)}, f32[8]{0:T(128)}, u32[]{:S(2)}) copy-start(f32[8]{0:T(128)} %param.10) | copy-start | bytes 100
  89.8 8.4 %copy-start.55 = (f32[8]{0:T(128)S(1)}, f32[8]{0:T(128)}, u32[]{:S(2)}) copy-start(f32[8]{0:T(128)} %param.9) | copy-start | bytes 100
  98.9 46.5 %all-to-all-start.1 = ((f32[16,1,12288]{2,1,0:T(1,128)}), f32[16,1,12288]{2,1,0:T(1,128)}, u32[]{:S(2)}, u32[]{:S(2)}) async-start(f32[16,1,12288]{2,1,0:T(1,128)} %reshape.521), calls=%async_computation.1 | async-start | bytes 1572864 | tf_op jit(solution)/shard_map/all_to_all | solution.py:113
  145.4 33.7 %all-to-all-start.4 = ((f32[16,1,12288]{2,1,0:T(1,128)}), f32[16,1,12288]{2,1,0:T(1,128)}, u32[]{:S(2)}, u32[]{:S(2)}) async-start(f32[16,1,12288]{2,1,0:T(1,128)} %reshape.515), calls=%async_computation.4 | async-start | bytes 1572864 | tf_op jit(solution)/shard_map/all_to_all | solution.py:119
  168.8 2.3 copy-start.28
  172.7 2.2 copy-start.11
  173.8 3.5 copy-start.7
  179.2 45.7 %all-to-all-start.5 = ((f32[16,1,12288]{2,1,0:T(1,128)}), f32[16,1,12288]{2,1,0:T(1,128)}, u32[]{:S(2)}, u32[]{:S(2)}) async-start(f32[16,1,12288]{2,1,0:T(1,128)} %reshape.513), calls=%async_computation.5 | async-start | bytes 1572864 | tf_op jit(solution)/shard_map/all_to_all | solution.py:120
  189.1 2.3 copy-start.30
  198.3 2.2 copy-start.10
  224.8 32.2 %all-to-all-start.2 = ((f32[16,1,12288]{2,1,0:T(1,128)}), f32[16,1,12288]{2,1,0:T(1,128)}, u32[]{:S(2)}, u32[]{:S(2)}) async-start(f32[16,1,12288]{2,1,0:T(1,128)} %reshape.527), calls=%async_computation.2 | async-start | bytes 1572864 | tf_op jit(solution)/shard_map/all_to_all | solution.py:126
  248.0 2.3 copy-start.29
  251.8 3.3 copy-start.12
  257.0 28.1 %all-to-all-start.3 = ((f32[16,1,12288]{2,1,0:T(1,128)}), f32[16,1,12288]{2,1,0:T(1,128)}, u32[]{:S(2)}, u32[]{:S(2)}) async-start(f32[16,1,12288]{2,1,0:T(1,128)} %reshape.525), calls=%async_computation.3 | async-start | bytes 1572864 | tf_op jit(solution)/shard_map/all_to_all | solution.py:127
  266.7 1.7 copy-start.44
  268.8 3.4 copy-start.8
  285.1 30.4 %all-to-all-start.7 = ((f32[16,1,12288]{2,1,0:T(1,128)}), f32[16,1,12288]{2,1,0:T(1,128)}, u32[]{:S(2)}, u32[]{:S(2)}) async-start(f32[16,1,12288]{2,1,0:T(1,128)} %reshape.517), calls=%async_computation.7 | async-start | bytes 1572864 | tf_op jit(solution)/shard_map/all_to_all | solution.py:129
  294.3 2.1 copy-start.6
  315.5 51.5 %all-to-all-start.6 = ((f32[16,1,12288]{2,1,0:T(1,128)}), f32[16,1,12288]{2,1,0:T(1,128)}, u32[]{:S(2)}, u32[]{:S(2)}) async-start(f32[16,1,12288]{2,1,0:T(1,128)} %reshape.519), calls=%async_computation.6 | async-start | bytes 1572864 | tf_op jit(solution)/shard_map/all_to_all | solution.py:128
  347.8 1.9 copy-start.3
  353.3 3.8 copy-start.1
  353.3 3.8 copy-start.34
  374.5 1.9 copy-start.2
  374.5 2.1 copy-start.32
  376.5 5.7 %copy-start.31 = (f32[128,3,8,64]{0,3,2,1:T(8,128)S(1)}, f32[128,3,8,64]{0,3,2,1:T(8,128)}, u32[]{:S(2)}) copy-start(f32[128,3,8,64]{0,3,2,1:T(8,128)} %fusion.12) | copy-start | bytes 2359300
  376.5 8.4 %copy-start.33 = (f32[128,3,8,64]{0,3,2,1:T(8,128)S(1)}, f32[128,3,8,64]{0,3,2,1:T(8,128)}, u32[]{:S(2)}) copy-start(f32[128,3,8,64]{0,3,2,1:T(8,128)} %fusion.10) | copy-start | bytes 2359300
  376.5 13.9 %copy-start.51 = (f32[8,128,128]{2,1,0:T(8,128)S(1)}, f32[8,128,128]{2,1,0:T(8,128)}, u32[]{:S(2)}) copy-start(f32[8,128,128]{2,1,0:T(8,128)} %get-tuple-element.17) | copy-start | bytes 1572868
  376.5 13.9 %copy-start.52 = (f32[8,128,128]{2,1,0:T(8,128)S(1)}, f32[8,128,128]{2,1,0:T(8,128)}, u32[]{:S(2)}) copy-start(f32[8,128,128]{2,1,0:T(8,128)} %fusion.92) | copy-start | bytes 1572868
  379.6 10.8 %copy-start.25 = (f32[1,3,8,127,128]{4,3,2,1,0:T(8,128)S(1)}, f32[1,3,8,127,128]{4,3,2,1,0:T(8,128)}, u32[]{:S(2)}) copy-start(f32[1,3,8,127,128]{4,3,2,1,0:T(8,128)} %get-tuple-element.43) | copy-start | bytes 4681732
  379.6 10.8 %copy-start.26 = (f32[3,8,128,128]{3,2,1,0:T(8,128)S(1)}, f32[3,8,128,128]{3,2,1,0:T(8,128)}, u32[]{:S(2)}) copy-start(f32[3,8,128,128]{3,2,1,0:T(8,128)} %fusion.97) | copy-start | bytes 4718596
  382.3 8.2 %copy-start.23 = (f32[1,3,8,128,1]{4,3,2,1,0:T(8,128)S(1)}, f32[1,3,8,128,1]{4,3,2,1,0:T(8,128)}, u32[]{:S(2)}) copy-start(f32[1,3,8,128,1]{4,3,2,1,0:T(8,128)} %get-tuple-element.41) | copy-start | bytes 36868
  382.3 8.2 %copy-start.24 = (f32[1,3,8,127,128]{4,3,2,1,0:T(8,128)S(1)}, f32[1,3,8,127,128]{4,3,2,1,0:T(8,128)}, u32[]{:S(2)}) copy-start(f32[1,3,8,127,128]{4,3,2,1,0:T(8,128)} %get-tuple-element.42) | copy-start | bytes 4681732
  385.0 5.5 %copy-start.21 = (f32[1,3,8,128,127]{4,3,2,1,0:T(8,128)S(1)}, f32[1,3,8,128,127]{4,3,2,1,0:T(8,128)}, u32[]{:S(2)}) copy-start(f32[1,3,8,128,127]{4,3,2,1,0:T(8,128)} %get-tuple-element.39) | copy-start | bytes 4681732
  385.0 5.5 %copy-start.22 = (f32[1,3,8,128,1]{4,3,2,1,0:T(8,128)S(1)}, f32[1,3,8,128,1]{4,3,2,1,0:T(8,128)}, u32[]{:S(2)}) copy-start(f32[1,3,8,128,1]{4,3,2,1,0:T(8,128)} %get-tuple-element.40) | copy-start | bytes 36868
  387.7 2.8 copy-start.20
  387.7 2.8 copy-start.53
  387.7 2.8 copy-start.56
  499.9 1.7 copy-start.27
  (21 other events, 25.6 us)
where the time goes:
time: 512 us; the launch traced here: 502 us
  local copies, waits for them, and re-layouts  146 us (29%)
  matrix products  96.8 us (19%)
  starting transfers between devices  88.5 us (17%)
  blocking collectives  85.6 us (17%)
  other arithmetic  74.7 us (15%)
  waiting for transfers between devices  6.08 us (1%)
    unnamed x142, local copies, waits for them, and re-layouts  78.5 us
    dot_general x24, matrix products, contract(): jnp.einsum(CONTRACT_FORMS[axis_dim], values, matrix, precision=lax.Precis...  68.9 us
    psum x1, blocking collectives, local(): lax.psum((jnp.sum(g_perp * unit_tangent, axis=sum_axes), part_next, part_...  45.1 us
    psum x1, blocking collectives, local(): tangent_sq = lax.psum(jnp.sum(tangent * tangent, axis=sum_axes), 'space')  40.5 us
    unnamed x16, matrix products  27.9 us
    all_to_all x1, starting transfers between devices, effective_field(): lax.all_to_all(spectra[1], 'space', split_axis=3, concat_axis=2, tiled=True)  12.7 us
    all_to_all x1, starting transfers between devices, effective_field(): lax.all_to_all(spectra[0], 'space', split_axis=3, concat_axis=2, tiled=True)  11.6 us
    another operation x4, local copies, waits for them, and re-layouts  11 us
  transfers between devices with their start and end apart: 12, of which 1 were waited for; matrix products, arithmetic and copies ran while one was open for 57% of the time, Pallas kernels for 0%

commit v1 on v0

v1 whole, which is shorter than its diff:
```python
import functools
import math

import jax
import jax.numpy as jnp
import numpy as np
from jax import lax
from jax.experimental import pallas as pl
from jax.experimental.pallas import tpu as pltpu
from jax.sharding import PartitionSpec as P

STEP_SIZE = 0.2
SPRING = 4.0
EPSILON = 1e-06
TENSOR_ROWS = ((0, 3, 4), (3, 1, 5), (4, 5, 2))
G = 128
HALF = G // 2
SLABS = 16
PLANES = G // SLABS
PARTS = 2
ROWS = PLANES // PARTS * 8
BLOCK = SLABS * ROWS
MESH = pl.DeviceIdType.MESH
F32 = jnp.float32
BF16 = jnp.bfloat16


def pair(matrix):
    high = matrix.astype(BF16)
    low = (matrix - high.astype(np.float64)).astype(BF16)
    return np.stack([high, low])


def tables():
    index = np.arange(G)
    angle = 2.0 * math.pi * (np.outer(index, index) % G) / G
    cos, sin = np.cos(angle), np.sin(angle)
    z_there = np.concatenate([cos[:, :HALF], cos[:, HALF : HALF + 1], -sin[:, 1:HALF]], axis=1)
    z_back = np.concatenate(
        [cos[:1], 2.0 * cos[1:HALF], cos[HALF : HALF + 1], -2.0 * sin[1:HALF]], axis=0
    )
    order = index.reshape(SLABS, PARTS, PLANES // PARTS).transpose(1, 0, 2).reshape(-1)
    y_there = np.concatenate([cos[order], sin[order]], axis=0)
    y_back = np.concatenate([cos[:, order], -sin[:, order]], axis=1)
    x_there = np.concatenate([cos, sin], axis=1)
    x_back = np.concatenate([cos, -sin], axis=1)
    upper, edge = order > HALF, (order == 0) | (order == HALF)
    middle = ~upper & ~edge
    there = np.zeros((4, G, G), np.float32)
    there[0] = 1.0
    there[3, :, :HALF], there[3, :, HALF:] = -1.0, 1.0
    there[0, upper, 0] = 0.0
    there[0, ~edge, HALF] = 0.0
    there[1, upper, HALF] = 1.0
    there[2, upper, HALF] = -1.0
    there[3, :, HALF] = 0.0
    there[3, ~middle, 0] = 0.0
    back = np.zeros((4, G, G), np.float32)
    back[0] = 1.0
    back[3, :, :HALF], back[3, :, HALF:] = -1.0, 1.0
    back[0, :, 0] = np.where(edge, 1.0, np.where(middle, 2.0, 0.0))
    back[0, :, HALF] = np.where(edge, 1.0, 0.0)
    back[1, :, 0] = np.where(upper, 2.0, 0.0)
    back[2, :, HALF] = np.where(upper, 2.0, 0.0)
    back[3, :, HALF] = np.where(middle, 2.0, 0.0)
    back[3, :, 0] = 0.0
    return (
        pair(z_there),
        pair(y_there),
        pair(x_there),
        pair(x_back),
        pair(y_back),
        pair(z_back),
        there,
        back,
    )


def dot(left, right):
    return jnp.dot(left, right, preferred_element_type=F32)


def split(values):
    high = values.astype(BF16)
    return high, (values - high.astype(F32)).astype(BF16)


def by_left(table, values):
    high, low = split(values)
    return dot(table[0], high) + (dot(table[0], low) + dot(table[1], high))


def by_right(values, table):
    high, low = split(values)
    return dot(high, table[0]) + (dot(low, table[0]) + dot(high, table[1]))


def turned(values):
    return pltpu.roll(values, HALF, 1)


def angle(sine, cosine):
    size = jnp.abs(cosine)
    small, large = jnp.minimum(sine, size), jnp.maximum(sine, size)
    far = small > 0.41421356 * large
    top = jnp.where(far, small - large, small)
    bottom = jnp.where(far, small + large, large)
    ratio = top / jnp.where(large == 0.0, 1.0, bottom)
    square = ratio * ratio
    series = 8.05374449538e-2 * square - 1.38776856032e-1
    series = series * square + 1.99777106478e-1
    series = series * square - 3.33329491539e-1
    value = series * square * ratio + ratio
    value = value + jnp.where(far, math.pi / 4, 0.0)
    value = jnp.where(sine > size, math.pi / 2 - value, value)
    return jnp.where(cosine < 0.0, math.pi - value, value)


def squared_angle(first, second):
    cross_x = first[1] * second[2] - first[2] * second[1]
    cross_y = first[2] * second[0] - first[0] * second[2]
    cross_z = first[0] * second[1] - first[1] * second[0]
    sine = jnp.sqrt(cross_x * cross_x + cross_y * cross_y + cross_z * cross_z)
    cosine = first[0] * second[0] + first[1] * second[1] + first[2] * second[2]
    value = angle(sine, cosine)
    return value * value


def tile_sum(values):
    return jnp.sum(values.reshape(G // 8, 8, G), axis=0)


def row_sum(values):
    return jnp.sum(values, axis=0, keepdims=True)


def whole_sum(values):
    return jnp.sum(jnp.sum(values, axis=0, keepdims=True), axis=1, keepdims=True)


def kernel(
    moment_in,
    labels_in,
    tensor_in,
    anisotropy,
    stiffness,
    z_there,
    y_there,
    x_there,
    x_back,
    y_back,
    z_back,
    there,
    back,
    path_out,
    force_out,
    moment,
    labels,
    tensor,
    packed,
    sending,
    spectrum,
    answer,
    arrived,
    preceding,
    following,
    tangent,
    field,
    path,
    force,
    sums_sent,
    sums,
    load_sem,
    there_sent,
    there_got,
    back_sent,
    back_got,
    halo_sent,
    halo_got,
    image_sent,
    image_got,
    sums_out,
    sums_got,
    store_sem,
):
    image, slab = lax.axis_index("image"), lax.axis_index("space")
    images = lax.axis_size("image")
    other = lax.rem(image + images // 2, images)
    has_preceding, has_following = image > 0, image < images - 1
    next_slab, last_slab = lax.rem(slab + 1, SLABS), lax.rem(slab + SLABS - 1, SLABS)

    def device(of_image, of_slab):
        return {"image": of_image, "space": of_slab}

    barrier = pltpu.get_barrier_semaphore()

    @pl.loop(0, SLABS)
    def _(step):
        pl.semaphore_signal(barrier, inc=1, device_id=device(other, step), device_id_type=MESH)

    @pl.loop(1, SLABS)
    def _(step):
        target = lax.rem(slab + step, SLABS)
        pl.semaphore_signal(barrier, inc=1, device_id=device(image, target), device_id_type=MESH)

    @pl.when(has_preceding)
    def _():
        pl.semaphore_signal(barrier, inc=1, device_id=device(image - 1, slab), device_id_type=MESH)

    @pl.when(has_following)
    def _():
        pl.semaphore_signal(barrier, inc=1, device_id=device(image + 1, slab), device_id_type=MESH)

    loads = [
        pltpu.make_async_copy(
            moment_in.at[0, c], moment.at[c, pl.ds(1, PLANES)], load_sem.at[c]
        )
        for c in range(3)
    ]
    tensor_load = pltpu.make_async_copy(tensor_in, tensor, load_sem.at[3])
    labels_load = pltpu.make_async_copy(labels_in, labels, load_sem.at[4])
    for load in loads:
        load.start()
    tensor_load.start()
    labels_load.start()

    @pl.when(jnp.logical_not(has_preceding))
    def _():
        preceding[...] = jnp.zeros_like(preceding)

    @pl.when(jnp.logical_not(has_following))
    def _():
        following[...] = jnp.zeros_like(following)

    def send_there(c, part):
        @pl.loop(0, SLABS)
        def _(step):
            target = lax.rem(slab + step, SLABS)
            pltpu.make_async_remote_copy(
                src_ref=sending.at[c, pl.ds(part * BLOCK + target * ROWS, ROWS)],
                dst_ref=spectrum.at[c, part, slab],
                send_sem=there_sent.at[c, part],
                recv_sem=there_got.at[c, part],
                device_id=device(other, target),
                device_id_type=MESH,
            ).start()

    def send_back(c, part):
        @pl.loop(0, SLABS)
        def _(step):
            target = lax.rem(slab + step, SLABS)
            pltpu.make_async_remote_copy(
                src_ref=answer.at[c, part, target],
                dst_ref=arrived.at[c, pl.ds(part * BLOCK + slab * ROWS, ROWS)],
                send_sem=back_sent.at[c, part],
                recv_sem=back_got.at[c, part],
                device_id=device(other, target),
                device_id_type=MESH,
            ).start()

    def whole_there(c, part):
        return pltpu.make_async_copy(
            sending.at[c, pl.ds(part * BLOCK, BLOCK)],
            sending.at[c, pl.ds(part * BLOCK, BLOCK)],
            there_sent.at[c, part],
        )

    def whole_spectrum(c, part):
        return pltpu.make_async_copy(
            spectrum.at[c, part], spectrum.at[c, part], there_got.at[c, part]
        )

    def whole_back(c, part):
        return pltpu.make_async_copy(
            answer.at[c, part], answer.at[c, part], back_sent.at[c, part]
        )

    def whole_arrived(c, part):
        return pltpu.make_async_copy(
            arrived.at[c, pl.ds(part * BLOCK, BLOCK)],
            arrived.at[c, pl.ds(part * BLOCK, BLOCK)],
            back_got.at[c, part],
        )

    for c in range(3):
        loads[c].wait()

        @pl.loop(0, PLANES // 2)
        def _(step):
            cells = moment[c, pl.ds(1 + 2 * step, 2)].reshape(2 * G, G)
            lines = by_right(cells, z_there)
            both = by_left(y_there, jnp.concatenate([lines[:G], lines[G:]], axis=1))
            for j in range(2):
                cosine, sine = both[:G, j * G : (j + 1) * G], both[G:, j * G : (j + 1) * G]
                values = there[0] * cosine + there[2] * sine
                values = values + turned(there[1] * cosine + there[3] * sine)
                sending[c, pl.ds(2 * step + j, G, stride=8), :] = values

        if c == 0:
            pl.semaphore_wait(
                barrier, 2 * SLABS - 1 + has_preceding.astype(jnp.int32) + has_following.astype(jnp.int32)
            )
        send_there(c, 0)

    for part in range(1, PARTS):
        for c in range(3):
            send_there(c, part)

    halo = [
        pltpu.make_async_remote_copy(
            src_ref=moment.at[:, source],
            dst_ref=moment.at[:, target],
            send_sem=halo_sent.at[n],
            recv_sem=halo_got.at[n],
            device_id=device(image, to),
            device_id_type=MESH,
        )
        for n, (source, target, to) in enumerate(
            ((PLANES, 0, next_slab), (1, PLANES + 1, last_slab))
        )
    ]
    for copy in halo:
        copy.start()
    own = moment.at[:, pl.ds(1, PLANES)]
    to_following = pltpu.make_async_remote_copy(
        src_ref=own,
        dst_ref=preceding,
        send_sem=image_sent.at[0],
        recv_sem=image_got.at[0],
        device_id=device(lax.rem(image + 1, images), slab),
        device_id_type=MESH,
    )
    to_preceding = pltpu.make_async_remote_copy(
        src_ref=own,
        dst_ref=following,
        send_sem=image_sent.at[1],
        recv_sem=image_got.at[1],
        device_id=device(lax.rem(image + images - 1, images), slab),
        device_id_type=MESH,
    )

    @pl.when(has_following)
    def _():
        to_following.start()

    @pl.when(has_preceding)
    def _():
        to_preceding.start()

    tensor_load.wait()
    lane = lax.broadcasted_iota(jnp.int32, (G, G), 1)

    @pl.loop(0, PLANES)
    def _(row):
        wave = slab * PLANES + row
        first = jnp.logical_and(lane == 0, wave <= HALF)
        middle = jnp.logical_and(lane == HALF, jnp.logical_or(wave == 0, wave >= HALF))
        plain = jnp.logical_and(lane > 0, lane < HALF)
        keep = jnp.logical_or(jnp.logical_or(first, middle), plain)
        for n in range(6):
            values = tensor[n, pl.ds(row, G, stride=8), :]
            packed[n, row] = jnp.where(keep, values, turned(values)) * (-1.0 / G**3)

    labels_load.wait()
    for copy in halo:
        copy.wait()

    @pl.loop(0, PLANES)
    def _(plane):
        region = labels[plane]
        stiff_cell = jnp.zeros((G, G), F32)
        anis_cell = jnp.zeros((G, G), F32)
        for n in range(8):
            stiff_cell = jnp.where(region == n, stiffness[n], stiff_cell)
            anis_cell = jnp.where(region == n, anisotropy[n], anis_cell)
        for c in range(3):
            here = moment[c, plane + 1]
            around = moment[c, plane] + moment[c, plane + 2] - 6.0 * here
            around = around + pltpu.roll(here, 1, 0) + pltpu.roll(here, G - 1, 0)
            around = around + pltpu.roll(here, 1, 1) + pltpu.roll(here, G - 1, 1)
            value = stiff_cell * around
            if c == 2:
                value = value + 2.0 * anis_cell * here
            field[c, plane] = value

    real_column = jnp.logical_and(lane % HALF == 0, lax.rem(slab, SLABS // 2) == 0)
    sign = jnp.where(lane < HALF, 1.0, -1.0)

    def multiply(part):
        for c in range(3):
            whole_spectrum(c, part).wait()

        def row_of(row, first):
            def partner(values, factor):
                result = sign * turned(values)
                if first:
                    result = jnp.where(real_column, factor * values, result)
                return result

            at = pl.ds(pl.multiple_of(row * 8, 8), 8)
            lines = [spectrum[c, part, :, at, :].reshape(G, G) for c in range(3)]
            stack = jnp.concatenate(
                [jnp.concatenate([v, partner(v, 1.0)], axis=0) for v in lines], axis=1
            )
            waves = by_left(x_there, stack)
            waves = [waves[:, b * G : (b + 1) * G] for b in range(3)]
            at_row = part * (PLANES // PARTS) + row
            products = []
            for n in TENSOR_ROWS:
                value = packed[n[0], at_row] * waves[0]
                value = value + packed[n[1], at_row] * waves[1]
                products.append(value + packed[n[2], at_row] * waves[2])
            stack = jnp.concatenate(
                [jnp.concatenate([v, partner(v, -1.0)], axis=0) for v in products], axis=1
            )
            result = by_left(x_back, stack)
            for c in range(3):
                answer[c, part, :, at, :] = result[:, c * G : (c + 1) * G].reshape(SLABS, 8, G)

        first = part == 0
        if first:
            row_of(0, True)

        @pl.loop(1 if first else 0, PLANES // PARTS)
        def _(row):
            row_of(row, False)

        for c in range(3):
            send_back(c, part)

    multiply(0)

    @pl.when(has_preceding)
    def _():
        to_following.wait_recv()

    @pl.when(has_following)
    def _():
        to_preceding.wait_recv()

    def tangent_step(plane, carry):
        here = [moment[c, plane + 1] for c in range(3)]
        before = [preceding[c, plane] for c in range(3)]
        after = [following[c, plane] for c in range(3)]
        change = [after[c] - before[c] for c in range(3)]
        along = change[0] * here[0] + change[1] * here[1] + change[2] * here[2]
        change = [change[c] - along * here[c] for c in range(3)]
        for c in range(3):
            tangent[c, plane] = change[c]
        size = change[0] * change[0] + change[1] * change[1] + change[2] * change[2]
        return (
            carry[0] + tile_sum(size),
            carry[1] + tile_sum(squared_angle(here, after)),
            carry[2] + tile_sum(squared_angle(before, here)),
        )

    zero = jnp.zeros((8, G), F32)
    totals = lax.fori_loop(0, PLANES, tangent_step, (zero, zero, zero))

    def spread(n):
        @pl.loop(1, SLABS)
        def _(step):
            pltpu.make_async_remote_copy(
                src_ref=sums_sent.at[n],
                dst_ref=sums.at[n, step - 1],
                send_sem=sums_out.at[n],
                recv_sem=sums_got.at[n],
                device_id=device(image, lax.rem(slab + step, SLABS)),
                device_id_type=MESH,
            ).start()

    def collect(n):
        pltpu.make_async_copy(sums.at[n], sums.at[n], sums_got.at[n]).wait()
        return sums_sent[n] + jnp.sum(sums[n], axis=0)

    row = lax.broadcasted_iota(jnp.int32, (8, G), 0)
    rows = [jnp.broadcast_to(row_sum(value), (8, G)) for value in totals]
    sums_sent[0] = jnp.where(row == 0, rows[0], jnp.where(row == 1, rows[1], rows[2]))
    spread(0)

    for part in range(1, PARTS):
        multiply(part)

    for c in range(3):
        for part in range(PARTS):
            whole_arrived(c, part).wait()

        @pl.loop(0, PLANES // 2)
        def _(step):
            stack = []
            for j in range(2):
                values = arrived[c, pl.ds(2 * step + j, G, stride=8), :]
                first = back[0] * values + turned(back[1] * values)
                second = back[2] * values + turned(back[3] * values)
                stack.append(jnp.concatenate([first, second], axis=0))
            lines = by_left(y_back, jnp.concatenate(stack, axis=1))
            cells = by_right(jnp.concatenate([lines[:, :G], lines[:, G:]], axis=0), z_back)
            at = pl.ds(2 * step, 2)
            field[c, at] = field[c, at] + cells.reshape(2, G, G)

    def slope_step(plane, carry):
        here = [moment[c, plane + 1] for c in range(3)]
        gradient = [-field[c, plane] for c in range(3)]
        along = gradient[0] * here[0] + gradient[1] * here[1] + gradient[2] * here[2]
        total = jnp.zeros((G, G), F32)
        for c in range(3):
            value = gradient[c] - along * here[c]
            field[c, plane] = value
            total = total + value * tangent[c, plane]
        return carry + tile_sum(total)

    sums_sent[1] = lax.fori_loop(0, PLANES, slope_step, zero)
    spread(1)
    cells = float(G**3)
    first_sums = collect(0)
    parts = [whole_sum(jnp.where(row == n, first_sums, 0.0)) for n in range(3)]
    slope_sum = whole_sum(collect(1))
    factor = jnp.sqrt(cells / (parts[0] + EPSILON))
    spring = SPRING * (jnp.sqrt(parts[1] / cells) - jnp.sqrt(parts[2] / cells))
    strength = (slope_sum * factor / cells + spring) * factor
    movable = jnp.where(jnp.logical_and(has_preceding, has_following), 1.0, 0.0)

    stores = []

    def final_step(plane, carry):
        stepped = []
        for c in range(3):
            value = movable * (strength * tangent[c, plane] - field[c, plane])
            force[c, plane] = value
            stepped.append(moment[c, plane + 1] + STEP_SIZE * value)
        size = stepped[0] * stepped[0] + stepped[1] * stepped[1] + stepped[2] * stepped[2]
        scale = lax.rsqrt(size)
        for c in range(3):
            path[c, plane] = stepped[c] * scale
        return carry

    chunk = PLANES // 4
    for n in range(4):
        lax.fori_loop(n * chunk, (n + 1) * chunk, final_step, 0)
        at = pl.ds(n * chunk, chunk)
        stores.append(
            pltpu.make_async_copy(path.at[:, at], path_out.at[0, :, at], store_sem.at[0, n])
        )
        stores.append(
            pltpu.make_async_copy(force.at[:, at], force_out.at[0, :, at], store_sem.at[1, n])
        )
        stores[-2].start()
        stores[-1].start()

    for part in range(PARTS):
        for c in range(3):
            whole_there(c, part).wait()
            whole_back(c, part).wait()

    @pl.when(has_following)
    def _():
        to_following.wait_send()

    @pl.when(has_preceding)
    def _():
        to_preceding.wait_send()

    for n in range(2):
        out = pltpu.make_async_copy(sums.at[n], sums.at[n], sums_out.at[n])
        out.wait()
    for store in stores:
        store.wait()


def local(magnetization, region_labels, demag_kernel, anisotropy, stiffness):
    block = (3, PLANES, G, G)
    shape = jax.ShapeDtypeStruct((1,) + block, F32)
    any_spec = pl.BlockSpec(memory_space=pl.ANY)
    smem_spec = pl.BlockSpec(memory_space=pltpu.SMEM)
    vmem_spec = pl.BlockSpec(memory_space=pltpu.VMEM)
    constants = [jnp.asarray(table) for table in tables()]
    dma = pltpu.SemaphoreType.DMA
    return pl.pallas_call(
        kernel,
        out_shape=(shape, shape),
        in_specs=[any_spec] * 3 + [smem_spec] * 2 + [vmem_spec] * len(constants),
        out_specs=(any_spec, any_spec),
        scratch_shapes=[
            pltpu.VMEM((3, PLANES + 2, G, G), F32),
            pltpu.VMEM((PLANES, G, G), jnp.int32),
            pltpu.VMEM((6, G * PLANES, G), F32),
            pltpu.VMEM((6, PLANES, G, G), F32),
            pltpu.VMEM((3, PARTS * BLOCK, G), F32),
            pltpu.VMEM((3, PARTS, SLABS, ROWS, G), F32),
            pltpu.VMEM((3, PARTS, SLABS, ROWS, G), F32),
            pltpu.VMEM((3, PARTS * BLOCK, G), F32),
            pltpu.VMEM(block, F32),
            pltpu.VMEM(block, F32),
            pltpu.VMEM(block, F32),
            pltpu.VMEM(block, F32),
            pltpu.VMEM(block, F32),
            pltpu.VMEM(block, F32),
            pltpu.VMEM((2, 8, G), F32),
            pltpu.VMEM((2, SLABS - 1, 8, G), F32),
            dma((5,)),
            dma((3, PARTS)),
            dma((3, PARTS)),
            dma((3, PARTS)),
            dma((3, PARTS)),
            dma((2,)),
            dma((2,)),
            dma((2,)),
            dma((2,)),
            dma((2,)),
            dma((2,)),
            dma((2, 4)),
        ],
        compiler_params=pltpu.CompilerParams(
            collective_id=0, has_side_effects=True, vmem_limit_bytes=48 * 2**20
        ),
    )(
        magnetization,
        region_labels,
        demag_kernel.reshape(6, G * PLANES, G),
        anisotropy,
        stiffness,
        *constants,
    )


def solution(mesh):
    in_specs = (
        P("image", None, "space", None, None),
        P("space", None, None),
        P(None, None, "space", None),
        P(),
        P(),
    )
    out_specs = (P("image", None, "space", None, None), P("image", None, "space", None, None))
    return jax.shard_map(local, mesh=mesh, in_specs=in_specs, out_specs=out_specs, check_vma=False)
```

time: 512 us -> 133 us (0.26); the launches traced: 502 us -> 132 us
  local copies, waits for them, and re-layouts: 146 us -> 11.8 us
  Pallas kernels: 0 us -> 119 us
  matrix products: 96.8 us -> 0 us
  starting transfers between devices: 88.5 us -> 0 us
  blocking collectives: 85.6 us -> 0 us
  other arithmetic: 74.7 us -> 0 us
  waiting for transfers between devices: 6.08 us -> 0 us
    pallas_call x0 -> x1, Pallas kernels: none -> 119 us  [local(): pl.pallas_call(kernel, out_shape=(shape, shape), in_specs=[any_spec] * 3...]
    psum x2 -> x0, blocking collectives: 85.6 us -> none  [the longest x1 45.1 us: local(): lax.psum((jnp.sum(g_perp * unit_tangent, axis=sum_axes), part_next, part_...]
    all_to_all x8 -> x0, starting transfers between devices: 80.8 us -> none  [the longest x1 12.7 us: effective_field(): lax.all_to_all(spectra[1], 'space', split_axis=3, concat_axis=2, tiled=True)]
    dot_general x24 -> x0, matrix products: 68.9 us -> none  [contract(): jnp.einsum(CONTRACT_FORMS[axis_dim], values, matrix, precision=lax.Precis...]
    unnamed x142 -> x24, local copies, waits for them, and re-layouts: 78.5 us -> 11.8 us
    all_to_all x8 -> x0, other arithmetic: 36.3 us -> none  [the longest x1 4.57 us: effective_field(): lax.all_to_all(spectra[0], 'space', split_axis=3, concat_axis=2, tiled=True)]
    unnamed x16 -> x0, matrix products: 27.9 us -> none
    all_to_all x13 -> x0, local copies, waits for them, and re-layouts: 21.3 us -> none  [the longest x3 3.57 us: effective_field(): lax.all_to_all(spectra[3], 'space', split_axis=3, concat_axis=2, tiled=True)]
  transfers between devices with their start and end apart: 12 -> 0, of which waited for: 1 -> 0; matrix products, arithmetic and copies ran while one was open for 57% -> 0% of each run, Pallas kernels for 0% -> 0%
where the time goes in v1:
time: 133 us; the launch traced here: 132 us
  Pallas kernels  119 us (89%)
  local copies, waits for them, and re-layouts  11.8 us (9%)
    pallas_call x1, Pallas kernels, local(): pl.pallas_call(kernel, out_shape=(shape, shape), in_specs=[any_spec] * 3...  119 us
    unnamed x24, local copies, waits for them, and re-layouts  11.8 us

profile of v1, /device:TPU:8, one launch (start us, length us, event | category | flops | bytes accessed | tf_op | source)
XLA Modules:
  0.0 131.8 jit_solution(1526017212647937933)
XLA Ops:
  0.6 0.0 copy-start
  0.6 1.0 copy-done
  1.7 0.0 copy-start.1
  1.7 0.9 copy-done.1
  2.6 0.0 copy-start.2
  2.6 0.9 copy-done.2
  3.6 0.0 copy-start.3
  3.6 0.9 copy-done.3
  4.5 0.0 copy-start.4
  4.5 0.9 copy-done.4
  5.4 0.0 copy-start.5
  5.4 0.9 copy-done.5
  6.3 0.0 copy-start.6
  6.3 0.9 copy-done.6
  7.2 0.0 copy-start.7
  7.2 0.8 copy-done.7
  8.0 0.0 copy-start.8
  8.0 0.8 copy-done.8
  8.9 0.0 copy-start.9
  8.9 0.7 copy-done.9
  9.5 0.0 copy-start.10
  9.5 0.7 copy-done.10
  10.2 119.3 %shard_map.140 = (f32[1,3,8,128,128]{4,3,2,1,0:T(8,128)S(1)}, f32[1,3,8,128,128]{4,3,2,1,0:T(8,128)S(1)}) custom-call(f32[1,3,8,128,128]{4,3,2,1,0:T(8,128)} %moment_in.1, s32[8,128,128]{2,1,0:T(8,128)S(1)} %copy-done, f32[6,1024,128]{2,1,0:T(8,128)} %bitcast.1, f32[8]{0:T(128)S(1)} %copy-done.9, f32[8]{0:T(128)S(1)} %copy-done.10, ...), custom_call_target="tpu_custom_call" | custom-call | tf_op jit(solution)/shard_map/pallas_call | solution.py:578
  129.5 1.1 copy.17
  130.6 1.1 copy.18
Async XLA Ops:
  0.6 1.0 copy-start
  1.7 0.9 copy-start.1
  2.6 0.9 copy-start.2
  3.6 0.9 copy-start.3
  4.5 0.9 copy-start.4
  5.4 0.9 copy-start.5
  6.3 0.9 copy-start.6
  7.2 0.8 copy-start.7
  8.0 0.8 copy-start.8
  8.9 0.7 copy-start.9
  9.5 0.7 copy-start.10

commit v2 on v1

--- a/solution.py
+++ b/solution.py
@@ -20,6 +20,9 @@
 PARTS = 2
 ROWS = PLANES // PARTS * 8
 BLOCK = SLABS * ROWS
+RELAYS = 3
+COLUMN = 4
+DEPTH = SLABS // COLUMN
 MESH = pl.DeviceIdType.MESH
 F32 = jnp.float32
 BF16 = jnp.bfloat16
@@ -41,9 +44,9 @@
     )
     order = index.reshape(SLABS, PARTS, PLANES // PARTS).transpose(1, 0, 2).reshape(-1)
     y_there = np.concatenate([cos[order], sin[order]], axis=0)
-    y_back = np.concatenate([cos[:, order], -sin[:, order]], axis=1)
-    x_there = np.concatenate([cos, sin], axis=1)
-    x_back = np.concatenate([cos, -sin], axis=1)
+    y_back = np.concatenate([cos[:, order], -sin[:, order]], axis=0)
+    x_there = np.concatenate([cos, sin], axis=0)
+    x_back = np.concatenate([cos, -sin], axis=0)
     upper, edge = order > HALF, (order == 0) | (order == HALF)
     middle = ~upper & ~edge
     there = np.zeros((4, G, G), np.float32)
@@ -67,11 +70,11 @@
     return (
         pair(z_there),
         pair(y_there),
+        there,
         pair(x_there),
         pair(x_back),
         pair(y_back),
         pair(z_back),
-        there,
         back,
     )
 
@@ -83,6 +86,10 @@
 def split(values):
     high = values.astype(BF16)
     return high, (values - high.astype(F32)).astype(BF16)
+
+
+def beside(table):
+    return [jnp.concatenate([table[n, :G], table[n, G:]], axis=1) for n in range(2)]
 
 
 def by_left(table, values):
@@ -142,18 +149,28 @@
     moment_in,
     labels_in,
     tensor_in,
+    anisotropy_in,
+    stiffness_in,
+    z_there_in,
+    y_there_in,
+    there_in,
+    x_there_in,
+    x_back_in,
+    y_back_in,
+    z_back_in,
+    back_in,
+    path_out,
+    force_out,
     anisotropy,
     stiffness,
     z_there,
     y_there,
+    there,
     x_there,
     x_back,
     y_back,
     z_back,
-    there,
     back,
-    path_out,
-    force_out,
     moment,
     labels,
     tensor,
@@ -168,6 +185,8 @@
     field,
     path,
     force,
+    relay,
+    relay_halo,
     sums_sent,
     sums,
     load_sem,
@@ -179,6 +198,8 @@
     halo_got,
     image_sent,
     image_got,
+    relay_sent,
+    relay_got,
     sums_out,
     sums_got,
     store_sem,
@@ -211,6 +232,28 @@
     def _():
         pl.semaphore_signal(barrier, inc=1, device_id=device(image + 1, slab), device_id_type=MESH)
 
+    middle = images // 2
+    left_end, right_end = image == middle - 1, image == middle
+    is_end = jnp.logical_or(left_end, right_end)
+    left_relay = jnp.logical_and(image < middle - 1, lax.rem(image, 2) == 1)
+    right_relay = jnp.logical_and(image > middle, lax.rem(image, 2) == 0)
+    is_relay = jnp.logical_or(left_relay, right_relay)
+
+    @pl.when(is_end)
+    def _():
+        for n in range(RELAYS):
+            for target in (2 * n + 1, middle + 2 * n + 2):
+                pl.semaphore_signal(
+                    barrier, inc=1, device_id=device(target, slab), device_id_type=MESH
+                )
+
+    @pl.when(is_relay)
+    def _():
+        for target in (middle - 1, middle):
+            pl.semaphore_signal(
+                barrier, inc=1, device_id=device(target, slab), device_id_type=MESH
+            )
+
     loads = [
         pltpu.make_async_copy(
             moment_in.at[0, c], moment.at[c, pl.ds(1, PLANES)], load_sem.at[c]
@@ -219,10 +262,28 @@
     ]
     tensor_load = pltpu.make_async_copy(tensor_in, tensor, load_sem.at[3])
     labels_load = pltpu.make_async_copy(labels_in, labels, load_sem.at[4])
-    for load in loads:
+    early = [
+        pltpu.make_async_copy(source, target, load_sem.at[5 + n])
+        for n, (source, target) in enumerate(
+            ((z_there_in, z_there), (y_there_in, y_there), (there_in, there))
+        )
+    ]
+    late = [
+        pltpu.make_async_copy(source, target, load_sem.at[8 + n])
+        for n, (source, target) in enumerate(
+            (
+                (x_there_in, x_there),
+                (x_back_in, x_back),
+                (y_back_in, y_back),
+                (z_back_in, z_back),
+                (back_in, back),
+                (anisotropy_in, anisotropy),
+                (stiffness_in, stiffness),
+            )
+        )
+    ]
+    for load in loads[:1] + early + loads[1:] + [tensor_load] + late + [labels_load]:
         load.start()
-    tensor_load.start()
-    labels_load.start()
 
     @pl.when(jnp.logical_not(has_preceding))
     def _():
@@ -282,8 +343,187 @@
             back_got.at[c, part],
         )
 
+    def remote(source, target, sent, got, of_image, of_slab):
+        return pltpu.make_async_remote_copy(
+            src_ref=source,
+            dst_ref=target,
+            send_sem=sent,
+            recv_sem=got,
+            device_id=device(of_image, of_slab),
+            device_id_type=MESH,
+        )
+
+    high, low = slab // COLUMN, lax.rem(slab, COLUMN)
+    next_high, last_high = lax.rem(high + 1, DEPTH), lax.rem(high + DEPTH - 1, DEPTH)
+    at_top, at_bottom = low == COLUMN - 1, low == 0
+    strip = G // COLUMN
+
+    def strip_of(plane, n):
+        return moment.at[:, plane, pl.ds(n * strip, strip)]
+
+    up_whole = remote(
+        moment.at[:, PLANES], moment.at[:, 0], halo_sent.at[0], halo_got.at[0], image, next_slab
+    )
+    down_whole = remote(
+        moment.at[:, 1], moment.at[:, PLANES + 1], halo_sent.at[1], halo_got.at[1], image, last_slab
+    )
+    up_relay = remote(
+        relay_halo.at[0],
+        moment.at[:, 0, pl.ds(low * strip, strip)],
+        relay_sent.at[1],
+        halo_got.at[0],
+        image,
+        next_high * COLUMN,
+    )
+    down_relay = remote(
+        relay_halo.at[1],
+        moment.at[:, PLANES + 1, pl.ds(low * strip, strip)],
+        relay_sent.at[2],
+        halo_got.at[1],
+        image,
+        last_high * COLUMN + COLUMN - 1,
+    )
+    own = moment.at[:, pl.ds(1, PLANES)]
+    to_following = remote(
+        own, preceding, image_sent.at[0], image_got.at[0], lax.rem(image + 1, images), slab
+    )
+    to_preceding = remote(
+        own, following, image_sent.at[1], image_got.at[1], lax.rem(image + images - 1, images), slab
+    )
+    share = PLANES // (RELAYS + 1)
+    quarter = lax.rem(image, middle) // 2
+    right_forward = remote(
+        relay,
+        preceding.at[:, pl.ds(quarter * share, share)],
+        relay_sent.at[0],
+        image_got.at[0],
+        middle,
+        slab,
+    )
+    left_forward = remote(
+        relay,
+        following.at[:, pl.ds(quarter * share, share)],
+        relay_sent.at[0],
+        image_got.at[1],
+        middle - 1,
+        slab,
+    )
+
+    def quarter_of(n):
+        return moment.at[:, pl.ds(1 + n * share, share)]
+
+    def send_near():
+        @pl.when(left_end)
+        def _():
+            for n in range(RELAYS):
+                remote(
+                    quarter_of(n), relay, image_sent.at[0], relay_got.at[0], 2 * n + 1, slab
+                ).start()
+            remote(
+                quarter_of(RELAYS),
+                preceding.at[:, pl.ds(RELAYS * share, share)],
+                image_sent.at[0],
+                image_got.at[0],
+                middle,
+                slab,
+            ).start()
+
+        @pl.when(right_end)
+        def _():
+            for n in range(1, RELAYS + 1):
+                remote(
+                    quarter_of(n), relay, image_sent.at[1], relay_got.at[0], middle + 2 * n, slab
+                ).start()
+            remote(
+                quarter_of(0),
+                following.at[:, pl.ds(0, share)],
+                image_sent.at[1],
+                image_got.at[1],
+                middle - 1,
+                slab,
+            ).start()
+
+        @pl.when(at_top)
+        def _():
+            for n in range(COLUMN - 1):
+                remote(
+                    strip_of(PLANES, n),
+                    relay_halo.at[0],
+                    halo_sent.at[0],
+                    relay_got.at[1],
+                    image,
+                    high * COLUMN + n,
+                ).start()
+            remote(
+                strip_of(PLANES, COLUMN - 1),
+                strip_of(0, COLUMN - 1),
+                halo_sent.at[0],
+                halo_got.at[0],
+                image,
+                next_high * COLUMN,
+            ).start()
+
+        @pl.when(at_bottom)
+        def _():
+            for n in range(1, COLUMN):
+                remote(
+                    strip_of(1, n),
+                    relay_halo.at[1],
+                    halo_sent.at[1],
+                    relay_got.at[2],
+                    image,
+                    high * COLUMN + n,
+                ).start()
+            remote(
+                strip_of(1, 0),
+                strip_of(PLANES + 1, 0),
+                halo_sent.at[1],
+                halo_got.at[1],
+                image,
+                last_high * COLUMN + COLUMN - 1,
+            ).start()
+
+        @pl.when(jnp.logical_not(at_top))
+        def _():
+            up_whole.start()
+
+        @pl.when(jnp.logical_not(at_bottom))
+        def _():
+            down_whole.start()
+
+        @pl.when(jnp.logical_and(has_following, jnp.logical_not(left_end)))
+        def _():
+            to_following.start()
+
+        @pl.when(jnp.logical_and(has_preceding, jnp.logical_not(right_end)))
+        def _():
+            to_preceding.start()
+
+    def forward_relays():
+        @pl.when(jnp.logical_not(at_top))
+        def _():
+            pltpu.make_async_copy(relay_halo.at[0], relay_halo.at[0], relay_got.at[1]).wait()
+            up_relay.start()
+
+        @pl.when(jnp.logical_not(at_bottom))
+        def _():
+            pltpu.make_async_copy(relay_halo.at[1], relay_halo.at[1], relay_got.at[2]).wait()
+            down_relay.start()
+
+        @pl.when(left_relay)
+        def _():
+            pltpu.make_async_copy(relay, relay, relay_got.at[0]).wait()
+            right_forward.start()
+
+        @pl.when(right_relay)
+        def _():
+            pltpu.make_async_copy(relay, relay, relay_got.at[0]).wait()
+            left_forward.start()
+
     for c in range(3):
-        loads[c].wait()
+        if c == 0:
+            for load in [loads[0]] + early:
+                load.wait()
 
         @pl.loop(0, PLANES // 2)
         def _(step):
@@ -297,57 +537,24 @@
                 sending[c, pl.ds(2 * step + j, G, stride=8), :] = values
 
         if c == 0:
-            pl.semaphore_wait(
-                barrier, 2 * SLABS - 1 + has_preceding.astype(jnp.int32) + has_following.astype(jnp.int32)
-            )
+            signals = 2 * SLABS - 1 + has_preceding.astype(jnp.int32)
+            signals = signals + has_following.astype(jnp.int32) + 2 * is_relay.astype(jnp.int32)
+            pl.semaphore_wait(barrier, signals + 2 * RELAYS * is_end.astype(jnp.int32))
         send_there(c, 0)
+        if c == 0:
+            for load in loads[1:]:
+                load.wait()
+            send_near()
 
     for part in range(1, PARTS):
         for c in range(3):
             send_there(c, part)
 
-    halo = [
-        pltpu.make_async_remote_copy(
-            src_ref=moment.at[:, source],
-            dst_ref=moment.at[:, target],
-            send_sem=halo_sent.at[n],
-            recv_sem=halo_got.at[n],
-            device_id=device(image, to),
-            device_id_type=MESH,
-        )
-        for n, (source, target, to) in enumerate(
-            ((PLANES, 0, next_slab), (1, PLANES + 1, last_slab))
-        )
-    ]
-    for copy in halo:
-        copy.start()
-    own = moment.at[:, pl.ds(1, PLANES)]
-    to_following = pltpu.make_async_remote_copy(
-        src_ref=own,
-        dst_ref=preceding,
-        send_sem=image_sent.at[0],
-        recv_sem=image_got.at[0],
-        device_id=device(lax.rem(image + 1, images), slab),
-        device_id_type=MESH,
-    )
-    to_preceding = pltpu.make_async_remote_copy(
-        src_ref=own,
-        dst_ref=following,
-        send_sem=image_sent.at[1],
-        recv_sem=image_got.at[1],
-        device_id=device(lax.rem(image + images - 1, images), slab),
-        device_id_type=MESH,
-    )
-
-    @pl.when(has_following)
-    def _():
-        to_following.start()
-
-    @pl.when(has_preceding)
-    def _():
-        to_preceding.start()
+    forward_relays()
 
     tensor_load.wait()
+    for load in late:
+        load.wait()
     lane = lax.broadcasted_iota(jnp.int32, (G, G), 1)
 
     @pl.loop(0, PLANES)
@@ -361,9 +568,57 @@
             values = tensor[n, pl.ds(row, G, stride=8), :]
             packed[n, row] = jnp.where(keep, values, turned(values)) * (-1.0 / G**3)
 
+    real_column = jnp.logical_and(lane % HALF == 0, lax.rem(slab, SLABS // 2) == 0)
+    sign = jnp.where(lane < HALF, 1.0, -1.0)
+
+    def multiply(part):
+        for c in range(3):
+            whole_spectrum(c, part).wait()
+
+        def row_of(row, first):
+            def partner(values, factor):
+                result = sign * turned(values)
+                if first:
+                    result = jnp.where(real_column, factor * values, result)
+                return result
+
+            at = pl.ds(pl.multiple_of(row * 8, 8), 8)
+            lines = [spectrum[c, part, :, at, :].reshape(G, G) for c in range(3)]
+            stack = jnp.concatenate(
+                [jnp.concatenate([v, partner(v, 1.0)], axis=0) for v in lines], axis=1
+            )
+            waves = by_left(beside(x_there), stack)
+            waves = [waves[:, b * G : (b + 1) * G] for b in range(3)]
+            at_row = part * (PLANES // PARTS) + row
+            products = []
+            for n in TENSOR_ROWS:
+                value = packed[n[0], at_row] * waves[0]
+                value = value + packed[n[1], at_row] * waves[1]
+                products.append(value + packed[n[2], at_row] * waves[2])
+            stack = jnp.concatenate(
+                [jnp.concatenate([v, partner(v, -1.0)], axis=0) for v in products], axis=1
+            )
+            result = by_left(beside(x_back), stack)
+            for c in range(3):
+                answer[c, part, :, at, :] = result[:, c * G : (c + 1) * G].reshape(SLABS, 8, G)
+
+        first = part == 0
+        if first:
+            row_of(0, True)
+
+        @pl.loop(1 if first else 0, PLANES // PARTS)
+        def _(row):
+            row_of(row, False)
+
+        for c in range(3):
+            send_back(c, part)
+
+    for part in range(PARTS):
+        multiply(part)
+
     labels_load.wait()
-    for copy in halo:
-        copy.wait()
+    up_whole.wait_recv()
+    down_whole.wait_recv()
 
     @pl.loop(0, PLANES)
     def _(plane):
@@ -383,53 +638,6 @@
                 value = value + 2.0 * anis_cell * here
             field[c, plane] = value
 
-    real_column = jnp.logical_and(lane % HALF == 0, lax.rem(slab, SLABS // 2) == 0)
-    sign = jnp.where(lane < HALF, 1.0, -1.0)
-
-    def multiply(part):
-        for c in range(3):
-            whole_spectrum(c, part).wait()
-
-        def row_of(row, first):
-            def partner(values, factor):
-                result = sign * turned(values)
-                if first:
-                    result = jnp.where(real_column, factor * values, result)
-                return result
-
-            at = pl.ds(pl.multiple_of(row * 8, 8), 8)
-            lines = [spectrum[c, part, :, at, :].reshape(G, G) for c in range(3)]
-            stack = jnp.concatenate(
-                [jnp.concatenate([v, partner(v, 1.0)], axis=0) for v in lines], axis=1
-            )
-            waves = by_left(x_there, stack)
-            waves = [waves[:, b * G : (b + 1) * G] for b in range(3)]
-            at_row = part * (PLANES // PARTS) + row
-            products = []
-            for n in TENSOR_ROWS:
-                value = packed[n[0], at_row] * waves[0]
-                value = value + packed[n[1], at_row] * waves[1]
-                products.append(value + packed[n[2], at_row] * waves[2])
-            stack = jnp.concatenate(
-                [jnp.concatenate([v, partner(v, -1.0)], axis=0) for v in products], axis=1
-            )
-            result = by_left(x_back, stack)
-            for c in range(3):
-                answer[c, part, :, at, :] = result[:, c * G : (c + 1) * G].reshape(SLABS, 8, G)
-
-        first = part == 0
-        if first:
-            row_of(0, True)
-
-        @pl.loop(1 if first else 0, PLANES // PARTS)
-        def _(row):
-            row_of(row, False)
-
-        for c in range(3):
-            send_back(c, part)
-
-    multiply(0)
-
     @pl.when(has_preceding)
     def _():
         to_following.wait_recv()
@@ -478,9 +686,6 @@
     sums_sent[0] = jnp.where(row == 0, rows[0], jnp.where(row == 1, rows[1], rows[2]))
     spread(0)
 
-    for part in range(1, PARTS):
-        multiply(part)
-
     for c in range(3):
         for part in range(PARTS):
             whole_arrived(c, part).wait()
@@ -493,7 +698,7 @@
                 first = back[0] * values + turned(back[1] * values)
                 second = back[2] * values + turned(back[3] * values)
                 stack.append(jnp.concatenate([first, second], axis=0))
-            lines = by_left(y_back, jnp.concatenate(stack, axis=1))
+            lines = by_left(beside(y_back), jnp.concatenate(stack, axis=1))
             cells = by_right(jnp.concatenate([lines[:, :G], lines[:, G:]], axis=0), z_back)
             at = pl.ds(2 * step, 2)
             field[c, at] = field[c, at] + cells.reshape(2, G, G)
@@ -552,6 +757,25 @@
             whole_there(c, part).wait()
             whole_back(c, part).wait()
 
+    up_whole.wait_send()
+    down_whole.wait_send()
+
+    @pl.when(jnp.logical_not(at_top))
+    def _():
+        up_relay.wait_send()
+
+    @pl.when(jnp.logical_not(at_bottom))
+    def _():
+        down_relay.wait_send()
+
+    @pl.when(left_relay)
+    def _():
+        right_forward.wait_send()
+
+    @pl.when(right_relay)
+    def _():
+        left_forward.wait_send()
+
     @pl.when(has_following)
     def _():
         to_following.wait_send()
@@ -570,17 +794,18 @@
 def local(magnetization, region_labels, demag_kernel, anisotropy, stiffness):
     block = (3, PLANES, G, G)
     shape = jax.ShapeDtypeStruct((1,) + block, F32)
-    any_spec = pl.BlockSpec(memory_space=pl.ANY)
-    smem_spec = pl.BlockSpec(memory_space=pltpu.SMEM)
-    vmem_spec = pl.BlockSpec(memory_space=pltpu.VMEM)
+    hbm_spec = pl.BlockSpec(memory_space=pltpu.HBM)
     constants = [jnp.asarray(table) for table in tables()]
     dma = pltpu.SemaphoreType.DMA
     return pl.pallas_call(
         kernel,
         out_shape=(shape, shape),
-        in_specs=[any_spec] * 3 + [smem_spec] * 2 + [vmem_spec] * len(constants),
-        out_specs=(any_spec, any_spec),
+        in_specs=[hbm_spec] * (5 + len(constants)),
+        out_specs=(hbm_spec, hbm_spec),
         scratch_shapes=[
+            pltpu.SMEM((8,), F32),
+            pltpu.SMEM((8,), F32),
+            *(pltpu.VMEM(table.shape, table.dtype) for table in constants),
             pltpu.VMEM((3, PLANES + 2, G, G), F32),
             pltpu.VMEM((PLANES, G, G), jnp.int32),
             pltpu.VMEM((6, G * PLANES, G), F32),
@@ -595,9 +820,11 @@
             pltpu.VMEM(block, F32),
             pltpu.VMEM(block, F32),
             pltpu.VMEM(block, F32),
+            pltpu.VMEM((3, PLANES // (RELAYS + 1), G, G), F32),
+            pltpu.VMEM((2, 3, G // COLUMN, G), F32),
             pltpu.VMEM((2, 8, G), F32),
             pltpu.VMEM((2, SLABS - 1, 8, G), F32),
-            dma((5,)),
+            dma((15,)),
             dma((3, PARTS)),
             dma((3, PARTS)),
             dma((3, PARTS)),
@@ -606,12 +833,14 @@
             dma((2,)),
             dma((2,)),
             dma((2,)),
+            dma((3,)),
+            dma((3,)),
             dma((2,)),
             dma((2,)),
             dma((2, 4)),
         ],
         compiler_params=pltpu.CompilerParams(
-            collective_id=0, has_side_effects=True, vmem_limit_bytes=48 * 2**20
+            collective_id=0, has_side_effects=True, vmem_limit_bytes=63 * 2**20
         ),
     )(
         magnetization,

time: 133 us -> 104 us (0.78)
  Pallas kernels: 119 us -> 97.8 us
  local copies, waits for them, and re-layouts: 11.8 us -> 3.97 us
    pallas_call x1, Pallas kernels: 119 us -> 97.8 us  [local(): pl.pallas_call(kernel, out_shape=(shape, shape), in_specs=[hbm_spec] * (5...]
    unnamed x24 -> x4, local copies, waits for them, and re-layouts: 11.8 us -> 3.97 us
where the time goes in v2:
time: 104 us; the launch traced here: 102 us
  Pallas kernels  97.8 us (94%)
  local copies, waits for them, and re-layouts  3.97 us (4%)
    pallas_call x1, Pallas kernels, local(): pl.pallas_call(kernel, out_shape=(shape, shape), in_specs=[hbm_spec] * (5...  97.8 us
    unnamed x4, local copies, waits for them, and re-layouts  3.97 us

profile of v2, /device:TPU:8, one launch (start us, length us, event | category | flops | bytes accessed | tf_op | source)
XLA Modules:
  0.0 102.4 jit_solution(5430420746711706839)
XLA Ops:
  0.6 97.8 %shard_map.140 = (f32[1,3,8,128,128]{4,3,2,1,0:T(8,128)}, f32[1,3,8,128,128]{4,3,2,1,0:T(8,128)}) custom-call(f32[1,3,8,128,128]{4,3,2,1,0:T(8,128)} %moment_in.1, s32[8,128,128]{2,1,0:T(8,128)} %labels_in.1, f32[6,1024,128]{2,1,0:T(8,128)} %bitcast.1, f32[8]{0:T(128)} %anisotropy_in.1, f32[8]{0:T(128)} %stiffness_in.1, ...), custom_call_target="tpu_custom_call" | custom-call | tf_op jit(solution)/shard_map/pallas_call | solution.py:800
  98.4 0.0 copy-start
  98.4 2.8 %copy.17 = f32[1,3,8,128,128]{4,3,2,1,0:T(8,128)} copy(f32[1,3,8,128,128]{4,3,2,1,0:T(8,128)} %get-tuple-element.4) | data formatting | bytes 3145728
  101.2 0.0 copy-done
  101.2 1.1 %copy.18 = f32[1,3,8,128,128]{4,3,2,1,0:T(8,128)} copy(f32[1,3,8,128,128]{4,3,2,1,0:T(8,128)S(1)} %copy-done) | data formatting | bytes 3145728
Async XLA Ops:
  98.4 2.8 %copy-start = (f32[1,3,8,128,128]{4,3,2,1,0:T(8,128)S(1)}, f32[1,3,8,128,128]{4,3,2,1,0:T(8,128)}, u32[]{:S(2)}) copy-start(f32[1,3,8,128,128]{4,3,2,1,0:T(8,128)} %get-tuple-element.5) | copy-start | bytes 4718596

commit v3 on v2

--- a/solution.py
+++ b/solution.py
@@ -21,6 +21,8 @@
 ROWS = PLANES // PARTS * 8
 BLOCK = SLABS * ROWS
 RELAYS = 3
+STEPS = 4
+STEP_LIMIT = 24
 COLUMN = 4
 DEPTH = SLABS // COLUMN
 MESH = pl.DeviceIdType.MESH
@@ -32,6 +34,11 @@
     high = matrix.astype(BF16)
     low = (matrix - high.astype(np.float64)).astype(BF16)
     return np.stack([high, low])
+
+
+def square(matrix):
+    high, low = pair(matrix)
+    return np.stack([np.concatenate([high, high]), np.concatenate([low, 0 * low])])
 
 
 def tables():
@@ -68,13 +75,13 @@
     back[3, :, HALF] = np.where(middle, 2.0, 0.0)
     back[3, :, 0] = 0.0
     return (
-        pair(z_there),
+        square(z_there),
         pair(y_there),
         there,
         pair(x_there),
         pair(x_back),
         pair(y_back),
-        pair(z_back),
+        square(z_back),
         back,
     )
 
@@ -93,13 +100,17 @@
 
 
 def by_left(table, values):
+    rows = table[0].shape[0]
     high, low = split(values)
-    return dot(table[0], high) + (dot(table[0], low) + dot(table[1], high))
+    both = dot(jnp.concatenate([table[0], table[1]], axis=0), high)
+    return both[:rows] + (dot(table[0], low) + both[rows:])
 
 
 def by_right(values, table):
-    high, low = split(values)
-    return dot(high, table[0]) + (dot(low, table[0]) + dot(high, table[1]))
+    both = dot(
+        jnp.concatenate(split(values), axis=1), jnp.concatenate([table[0], table[1]], axis=1)
+    )
+    return both[:, :G] + both[:, G:]
 
 
 def turned(values):
@@ -159,8 +170,9 @@
     y_back_in,
     z_back_in,
     back_in,
-    path_out,
-    force_out,
+    field,
+    tangent,
+    strength_out,
     anisotropy,
     stiffness,
     z_there,
@@ -181,14 +193,12 @@
     arrived,
     preceding,
     following,
-    tangent,
-    field,
-    path,
-    force,
     relay,
     relay_halo,
     sums_sent,
     sums,
+    slope_sent,
+    slopes,
     load_sem,
     there_sent,
     there_got,
@@ -202,7 +212,6 @@
     relay_got,
     sums_out,
     sums_got,
-    store_sem,
 ):
     image, slab = lax.axis_index("image"), lax.axis_index("space")
     images = lax.axis_size("image")
@@ -665,33 +674,33 @@
     zero = jnp.zeros((8, G), F32)
     totals = lax.fori_loop(0, PLANES, tangent_step, (zero, zero, zero))
 
-    def spread(n):
+    def spread(source, targets, n):
         @pl.loop(1, SLABS)
         def _(step):
-            pltpu.make_async_remote_copy(
-                src_ref=sums_sent.at[n],
-                dst_ref=sums.at[n, step - 1],
-                send_sem=sums_out.at[n],
-                recv_sem=sums_got.at[n],
-                device_id=device(image, lax.rem(slab + step, SLABS)),
-                device_id_type=MESH,
+            remote(
+                source,
+                targets.at[step - 1],
+                sums_out.at[n],
+                sums_got.at[n],
+                image,
+                lax.rem(slab + step, SLABS),
             ).start()
 
-    def collect(n):
-        pltpu.make_async_copy(sums.at[n], sums.at[n], sums_got.at[n]).wait()
-        return sums_sent[n] + jnp.sum(sums[n], axis=0)
+    def collect(source, targets, n):
+        pltpu.make_async_copy(targets, targets, sums_got.at[n]).wait()
+        return source[...] + jnp.sum(targets[...], axis=0)
 
     row = lax.broadcasted_iota(jnp.int32, (8, G), 0)
     rows = [jnp.broadcast_to(row_sum(value), (8, G)) for value in totals]
-    sums_sent[0] = jnp.where(row == 0, rows[0], jnp.where(row == 1, rows[1], rows[2]))
-    spread(0)
-
+    sums_sent[...] = jnp.where(row == 0, rows[0], jnp.where(row == 1, rows[1], rows[2]))
+    spread(sums_sent, sums, 0)
+
+    slope = jnp.zeros((1, G), F32)
     for c in range(3):
         for part in range(PARTS):
             whole_arrived(c, part).wait()
 
-        @pl.loop(0, PLANES // 2)
-        def _(step):
+        def back_step(step, carry):
             stack = []
             for j in range(2):
                 values = arrived[c, pl.ds(2 * step + j, G, stride=8), :]
@@ -701,47 +710,94 @@
             lines = by_left(beside(y_back), jnp.concatenate(stack, axis=1))
             cells = by_right(jnp.concatenate([lines[:, :G], lines[:, G:]], axis=0), z_back)
             at = pl.ds(2 * step, 2)
-            field[c, at] = field[c, at] + cells.reshape(2, G, G)
-
-    def slope_step(plane, carry):
+            whole = field[c, at].reshape(2 * G, G) + cells
+            field[c, at] = whole.reshape(2, G, G)
+            return carry - row_sum(whole * tangent[c, at].reshape(2 * G, G))
+
+        slope = lax.fori_loop(0, PLANES // 2, back_step, slope)
+
+    slope_sent[...] = slope
+
+    spread(slope_sent, slopes, 1)
+
+    def normal_step(plane, carry):
         here = [moment[c, plane + 1] for c in range(3)]
         gradient = [-field[c, plane] for c in range(3)]
         along = gradient[0] * here[0] + gradient[1] * here[1] + gradient[2] * here[2]
-        total = jnp.zeros((G, G), F32)
         for c in range(3):
-            value = gradient[c] - along * here[c]
-            field[c, plane] = value
-            total = total + value * tangent[c, plane]
-        return carry + tile_sum(total)
-
-    sums_sent[1] = lax.fori_loop(0, PLANES, slope_step, zero)
-    spread(1)
+            field[c, plane] = gradient[c] - along * here[c]
+        return carry
+
+    lax.fori_loop(0, PLANES, normal_step, 0)
     cells = float(G**3)
-    first_sums = collect(0)
+    first_sums = collect(sums_sent, sums, 0)
     parts = [whole_sum(jnp.where(row == n, first_sums, 0.0)) for n in range(3)]
-    slope_sum = whole_sum(collect(1))
+    slope_sum = whole_sum(collect(slope_sent, slopes, 1))
     factor = jnp.sqrt(cells / (parts[0] + EPSILON))
     spring = SPRING * (jnp.sqrt(parts[1] / cells) - jnp.sqrt(parts[2] / cells))
     strength = (slope_sum * factor / cells + spring) * factor
-    movable = jnp.where(jnp.logical_and(has_preceding, has_following), 1.0, 0.0)
-
+    strength_out[...] = jnp.broadcast_to(strength, (1, G))
+
+    for part in range(PARTS):
+        for c in range(3):
+            whole_there(c, part).wait()
+            whole_back(c, part).wait()
+
+    up_whole.wait_send()
+    down_whole.wait_send()
+
+    @pl.when(jnp.logical_not(at_top))
+    def _():
+        up_relay.wait_send()
+
+    @pl.when(jnp.logical_not(at_bottom))
+    def _():
+        down_relay.wait_send()
+
+    @pl.when(left_relay)
+    def _():
+        right_forward.wait_send()
+
+    @pl.when(right_relay)
+    def _():
+        left_forward.wait_send()
+
+    @pl.when(has_following)
+    def _():
+        to_following.wait_send()
+
+    @pl.when(has_preceding)
+    def _():
+        to_preceding.wait_send()
+
+    pltpu.make_async_copy(sums, sums, sums_out.at[0]).wait()
+    pltpu.make_async_copy(slopes, slopes, sums_out.at[1]).wait()
+
+
+def step_kernel(
+    moment, normal, tangent, strength, path_out, force_out, path, force, store_sem
+):
+    image = lax.axis_index("image")
+    inside = jnp.logical_and(image > 0, image < lax.axis_size("image") - 1)
+    movable = jnp.where(inside, 1.0, 0.0)
+    chunk = PLANES // STEPS
     stores = []
-
-    def final_step(plane, carry):
+    factor = strength[...]
+
+    def plane_step(plane, carry):
         stepped = []
         for c in range(3):
-            value = movable * (strength * tangent[c, plane] - field[c, plane])
+            value = movable * (factor * tangent[c, plane] - normal[c, plane])
             force[c, plane] = value
-            stepped.append(moment[c, plane + 1] + STEP_SIZE * value)
+            stepped.append(moment[0, c, plane] + STEP_SIZE * value)
         size = stepped[0] * stepped[0] + stepped[1] * stepped[1] + stepped[2] * stepped[2]
         scale = lax.rsqrt(size)
         for c in range(3):
             path[c, plane] = stepped[c] * scale
         return carry
 
-    chunk = PLANES // 4
-    for n in range(4):
-        lax.fori_loop(n * chunk, (n + 1) * chunk, final_step, 0)
+    for n in range(STEPS):
+        lax.fori_loop(n * chunk, (n + 1) * chunk, plane_step, 0)
         at = pl.ds(n * chunk, chunk)
         stores.append(
             pltpu.make_async_copy(path.at[:, at], path_out.at[0, :, at], store_sem.at[0, n])
@@ -751,42 +807,6 @@
         )
         stores[-2].start()
         stores[-1].start()
-
-    for part in range(PARTS):
-        for c in range(3):
-            whole_there(c, part).wait()
-            whole_back(c, part).wait()
-
-    up_whole.wait_send()
-    down_whole.wait_send()
-
-    @pl.when(jnp.logical_not(at_top))
-    def _():
-        up_relay.wait_send()
-
-    @pl.when(jnp.logical_not(at_bottom))
-    def _():
-        down_relay.wait_send()
-
-    @pl.when(left_relay)
-    def _():
-        right_forward.wait_send()
-
-    @pl.when(right_relay)
-    def _():
-        left_forward.wait_send()
-
-    @pl.when(has_following)
-    def _():
-        to_following.wait_send()
-
-    @pl.when(has_preceding)
-    def _():
-        to_preceding.wait_send()
-
-    for n in range(2):
-        out = pltpu.make_async_copy(sums.at[n], sums.at[n], sums_out.at[n])
-        out.wait()
     for store in stores:
         store.wait()
 
@@ -795,13 +815,22 @@
     block = (3, PLANES, G, G)
     shape = jax.ShapeDtypeStruct((1,) + block, F32)
     hbm_spec = pl.BlockSpec(memory_space=pltpu.HBM)
+    vmem_spec = pl.BlockSpec(memory_space=pltpu.VMEM)
+
+    def in_hbm(array):
+        return pltpu.with_memory_space_constraint(array, pltpu.HBM)
+
     constants = [jnp.asarray(table) for table in tables()]
     dma = pltpu.SemaphoreType.DMA
-    return pl.pallas_call(
+    normal, tangent, strength = pl.pallas_call(
         kernel,
-        out_shape=(shape, shape),
+        out_shape=(
+            pltpu.VMEM(block, F32),
+            pltpu.VMEM(block, F32),
+            pltpu.VMEM((1, G), F32),
+        ),
         in_specs=[hbm_spec] * (5 + len(constants)),
-        out_specs=(hbm_spec, hbm_spec),
+        out_specs=(vmem_spec, vmem_spec, vmem_spec),
         scratch_shapes=[
             pltpu.SMEM((8,), F32),
             pltpu.SMEM((8,), F32),
@@ -816,14 +845,12 @@
             pltpu.VMEM((3, PARTS * BLOCK, G), F32),
             pltpu.VMEM(block, F32),
             pltpu.VMEM(block, F32),
-            pltpu.VMEM(block, F32),
-            pltpu.VMEM(block, F32),
-            pltpu.VMEM(block, F32),
-            pltpu.VMEM(block, F32),
             pltpu.VMEM((3, PLANES // (RELAYS + 1), G, G), F32),
             pltpu.VMEM((2, 3, G // COLUMN, G), F32),
-            pltpu.VMEM((2, 8, G), F32),
-            pltpu.VMEM((2, SLABS - 1, 8, G), F32),
+            pltpu.VMEM((8, G), F32),
+            pltpu.VMEM((SLABS - 1, 8, G), F32),
+            pltpu.VMEM((1, G), F32),
+            pltpu.VMEM((SLABS - 1, 1, G), F32),
             dma((15,)),
             dma((3, PARTS)),
             dma((3, PARTS)),
@@ -837,19 +864,26 @@
             dma((3,)),
             dma((2,)),
             dma((2,)),
-            dma((2, 4)),
         ],
         compiler_params=pltpu.CompilerParams(
-            collective_id=0, has_side_effects=True, vmem_limit_bytes=63 * 2**20
+            collective_id=0, has_side_effects=True, vmem_limit_bytes=40 * 2**20
         ),
     )(
-        magnetization,
-        region_labels,
-        demag_kernel.reshape(6, G * PLANES, G),
-        anisotropy,
-        stiffness,
-        *constants,
-    )
+        in_hbm(magnetization),
+        in_hbm(region_labels),
+        in_hbm(demag_kernel.reshape(6, G * PLANES, G)),
+        in_hbm(anisotropy),
+        in_hbm(stiffness),
+        *(in_hbm(constant) for constant in constants),
+    )
+    return pl.pallas_call(
+        step_kernel,
+        out_shape=(shape, shape),
+        in_specs=[vmem_spec] * 4,
+        out_specs=(hbm_spec, hbm_spec),
+        scratch_shapes=[pltpu.VMEM(block, F32)] * 2 + [dma((2, STEPS))],
+        compiler_params=pltpu.CompilerParams(vmem_limit_bytes=STEP_LIMIT * 2**20),
+    )(magnetization, normal, tangent, strength)
 
 
 def solution(mesh):

time: 104 us -> 98.6 us (0.948)
  local copies, waits for them, and re-layouts: 3.97 us -> 0.01 us
    unnamed x4 -> x2, local copies, waits for them, and re-layouts: 3.97 us -> 0.01 us
    pallas_call x1 -> x2, Pallas kernels: 97.8 us -> 96.9 us  [the longest x1 95 us: local(): pl.pallas_call(kernel, out_shape=(pltpu.VMEM(block, F32), pltpu.VMEM(bloc...]
where the time goes in v3:
time: 98.6 us; the launch traced here: 97.6 us
  Pallas kernels  96.9 us (98%)
    pallas_call x1, Pallas kernels, local(): pl.pallas_call(kernel, out_shape=(pltpu.VMEM(block, F32), pltpu.VMEM(bloc...  95 us

profile of v3, /device:TPU:8, one launch (start us, length us, event | category | flops | bytes accessed | tf_op | source)
XLA Modules:
  0.0 97.6 jit_solution(6179062696930041723)
XLA Ops:
  0.6 0.0 copy-start
  0.6 95.0 %shard_map.140 = (f32[3,8,128,128]{3,2,1,0:T(8,128)S(1)}, f32[3,8,128,128]{3,2,1,0:T(8,128)S(1)}, f32[1,128]{1,0:T(1,128)S(1)}) custom-call(f32[1,3,8,128,128]{4,3,2,1,0:T(8,128)} %moment.1, s32[8,128,128]{2,1,0:T(8,128)} %labels_in.1, f32[6,1024,128]{2,1,0:T(8,128)} %bitcast.1, f32[8]{0:T(128)} %anisotropy_in.1, f32[8]{0:T(128)} %stiffness_in.1, ...), custom_call_target="tpu_custom_call" | custom-call | tf_op jit(solution)/shard_map/pallas_call | solution.py:825
  95.7 0.0 copy-done
  95.7 1.9 %shard_map.141 = (f32[1,3,8,128,128]{4,3,2,1,0:T(8,128)}, f32[1,3,8,128,128]{4,3,2,1,0:T(8,128)}) custom-call(f32[1,3,8,128,128]{4,3,2,1,0:T(8,128)S(1)} %copy-done, f32[3,8,128,128]{3,2,1,0:T(8,128)S(1)} %get-tuple-element.5.normal, f32[3,8,128,128]{3,2,1,0:T(8,128)S(1)} %get-tuple-element.6.tangent, f32[1,128]{1,0:T(1,128)S(1)} %get-tuple-element.7.strength), custom_call_target="tpu_custom_call" | custom-call | tf_op jit(solution)/shard_map/pallas_call | solution.py:879
Async XLA Ops:
  0.6 95.1 %copy-start = (f32[1,3,8,128,128]{4,3,2,1,0:T(8,128)S(1)}, f32[1,3,8,128,128]{4,3,2,1,0:T(8,128)}, u32[]{:S(2)}) copy-start(f32[1,3,8,128,128]{4,3,2,1,0:T(8,128)} %moment.1) | copy-start | bytes 4718596

commit v4 on v3

--- a/solution.py
+++ b/solution.py
@@ -20,8 +20,8 @@
 PARTS = 2
 ROWS = PLANES // PARTS * 8
 BLOCK = SLABS * ROWS
-RELAYS = 3
-STEPS = 4
+RELAYS = PLANES - 1
+STEPS = 8
 STEP_LIMIT = 24
 COLUMN = 4
 DEPTH = SLABS // COLUMN
@@ -216,6 +216,7 @@
     image, slab = lax.axis_index("image"), lax.axis_index("space")
     images = lax.axis_size("image")
     other = lax.rem(image + images // 2, images)
+    other = other + 1 - 2 * lax.rem(other, 2)
     has_preceding, has_following = image > 0, image < images - 1
     next_slab, last_slab = lax.rem(slab + 1, SLABS), lax.rem(slab + SLABS - 1, SLABS)
 
@@ -226,7 +227,8 @@
 
     @pl.loop(0, SLABS)
     def _(step):
-        pl.semaphore_signal(barrier, inc=1, device_id=device(other, step), device_id_type=MESH)
+        target = lax.rem(slab + step, SLABS)
+        pl.semaphore_signal(barrier, inc=1, device_id=device(other, target), device_id_type=MESH)
 
     @pl.loop(1, SLABS)
     def _(step):
@@ -244,14 +246,13 @@
     middle = images // 2
     left_end, right_end = image == middle - 1, image == middle
     is_end = jnp.logical_or(left_end, right_end)
-    left_relay = jnp.logical_and(image < middle - 1, lax.rem(image, 2) == 1)
-    right_relay = jnp.logical_and(image > middle, lax.rem(image, 2) == 0)
+    left_relay, right_relay = image < middle - 1, image > middle
     is_relay = jnp.logical_or(left_relay, right_relay)
 
     @pl.when(is_end)
     def _():
         for n in range(RELAYS):
-            for target in (2 * n + 1, middle + 2 * n + 2):
+            for target in (n, middle + n + 1):
                 pl.semaphore_signal(
                     barrier, inc=1, device_id=device(target, slab), device_id_type=MESH
                 )
@@ -400,10 +401,10 @@
         own, following, image_sent.at[1], image_got.at[1], lax.rem(image + images - 1, images), slab
     )
     share = PLANES // (RELAYS + 1)
-    quarter = lax.rem(image, middle) // 2
+    turn = lax.rem(image, middle)
     right_forward = remote(
         relay,
-        preceding.at[:, pl.ds(quarter * share, share)],
+        preceding.at[:, pl.ds(turn * share, share)],
         relay_sent.at[0],
         image_got.at[0],
         middle,
@@ -411,14 +412,14 @@
     )
     left_forward = remote(
         relay,
-        following.at[:, pl.ds(quarter * share, share)],
+        following.at[:, pl.ds(turn * share, share)],
         relay_sent.at[0],
         image_got.at[1],
         middle - 1,
         slab,
     )
 
-    def quarter_of(n):
+    def share_of(n):
         return moment.at[:, pl.ds(1 + n * share, share)]
 
     def send_near():
@@ -426,10 +427,10 @@
         def _():
             for n in range(RELAYS):
                 remote(
-                    quarter_of(n), relay, image_sent.at[0], relay_got.at[0], 2 * n + 1, slab
+                    share_of(n), relay, image_sent.at[0], relay_got.at[0], n, slab
                 ).start()
             remote(
-                quarter_of(RELAYS),
+                share_of(RELAYS),
                 preceding.at[:, pl.ds(RELAYS * share, share)],
                 image_sent.at[0],
                 image_got.at[0],
@@ -441,10 +442,10 @@
         def _():
             for n in range(1, RELAYS + 1):
                 remote(
-                    quarter_of(n), relay, image_sent.at[1], relay_got.at[0], middle + 2 * n, slab
+                    share_of(n), relay, image_sent.at[1], relay_got.at[0], middle + n, slab
                 ).start()
             remote(
-                quarter_of(0),
+                share_of(0),
                 following.at[:, pl.ds(0, share)],
                 image_sent.at[1],
                 image_got.at[1],
@@ -508,7 +509,7 @@
         def _():
             to_preceding.start()
 
-    def forward_relays():
+    def forward_strips():
         @pl.when(jnp.logical_not(at_top))
         def _():
             pltpu.make_async_copy(relay_halo.at[0], relay_halo.at[0], relay_got.at[1]).wait()
@@ -519,6 +520,7 @@
             pltpu.make_async_copy(relay_halo.at[1], relay_halo.at[1], relay_got.at[2]).wait()
             down_relay.start()
 
+    def forward_image():
         @pl.when(left_relay)
         def _():
             pltpu.make_async_copy(relay, relay, relay_got.at[0]).wait()
@@ -559,7 +561,7 @@
         for c in range(3):
             send_there(c, part)
 
-    forward_relays()
+    forward_strips()
 
     tensor_load.wait()
     for load in late:
@@ -624,6 +626,8 @@
 
     for part in range(PARTS):
         multiply(part)
+        if part == 0:
+            forward_image()
 
     labels_load.wait()
     up_whole.wait_recv()
@@ -732,10 +736,10 @@
     cells = float(G**3)
     first_sums = collect(sums_sent, sums, 0)
     parts = [whole_sum(jnp.where(row == n, first_sums, 0.0)) for n in range(3)]
-    slope_sum = whole_sum(collect(slope_sent, slopes, 1))
     factor = jnp.sqrt(cells / (parts[0] + EPSILON))
     spring = SPRING * (jnp.sqrt(parts[1] / cells) - jnp.sqrt(parts[2] / cells))
-    strength = (slope_sum * factor / cells + spring) * factor
+    per_slope, constant = factor * factor / cells, spring * factor
+    strength = whole_sum(collect(slope_sent, slopes, 1)) * per_slope + constant
     strength_out[...] = jnp.broadcast_to(strength, (1, G))
 
     for part in range(PARTS):

time: 98.6 us -> 98.5 us (level)
  the two profiles are of different devices: /device:TPU:8 before, /device:TPU:1 now
where the time goes in v4:
time: 98.5 us; the launch traced here: 98.4 us
  Pallas kernels  97.8 us (99%)
    pallas_call x1, Pallas kernels, local(): pl.pallas_call(kernel, out_shape=(pltpu.VMEM(block, F32), pltpu.VMEM(bloc...  95.9 us

profile of v4, /device:TPU:1, one launch (start us, length us, event | category | flops | bytes accessed | tf_op | source)
XLA Modules:
  0.0 98.4 jit_solution(10443586794948044316)
XLA Ops:
  0.6 0.0 copy-start
  0.6 95.9 %shard_map.140 = (f32[3,8,128,128]{3,2,1,0:T(8,128)S(1)}, f32[3,8,128,128]{3,2,1,0:T(8,128)S(1)}, f32[1,128]{1,0:T(1,128)S(1)}) custom-call(f32[1,3,8,128,128]{4,3,2,1,0:T(8,128)} %moment.1, s32[8,128,128]{2,1,0:T(8,128)} %labels_in.1, f32[6,1024,128]{2,1,0:T(8,128)} %bitcast.1, f32[8]{0:T(128)} %anisotropy_in.1, f32[8]{0:T(128)} %stiffness_in.1, ...), custom_call_target="tpu_custom_call" | custom-call | tf_op jit(solution)/shard_map/pallas_call | solution.py:829
  96.6 0.0 copy-done
  96.6 1.9 %shard_map.141 = (f32[1,3,8,128,128]{4,3,2,1,0:T(8,128)}, f32[1,3,8,128,128]{4,3,2,1,0:T(8,128)}) custom-call(f32[1,3,8,128,128]{4,3,2,1,0:T(8,128)S(1)} %copy-done, f32[3,8,128,128]{3,2,1,0:T(8,128)S(1)} %get-tuple-element.5.normal, f32[3,8,128,128]{3,2,1,0:T(8,128)S(1)} %get-tuple-element.6.tangent, f32[1,128]{1,0:T(1,128)S(1)} %get-tuple-element.7.strength), custom_call_target="tpu_custom_call" | custom-call | tf_op jit(solution)/shard_map/pallas_call | solution.py:883
Async XLA Ops:
  0.6 95.9 %copy-start = (f32[1,3,8,128,128]{4,3,2,1,0:T(8,128)S(1)}, f32[1,3,8,128,128]{4,3,2,1,0:T(8,128)}, u32[]{:S(2)}) copy-start(f32[1,3,8,128,128]{4,3,2,1,0:T(8,128)} %moment.1) | copy-start | bytes 4718596

commit v5 on v4

--- a/solution.py
+++ b/solution.py
@@ -51,7 +51,9 @@
     )
     order = index.reshape(SLABS, PARTS, PLANES // PARTS).transpose(1, 0, 2).reshape(-1)
     y_there = np.concatenate([cos[order], sin[order]], axis=0)
-    y_back = np.concatenate([cos[:, order], -sin[:, order]], axis=0)
+    y_back = np.concatenate(
+        [np.concatenate([cos[:, o], -sin[:, o]], axis=1) for o in order.reshape(PARTS, -1)], axis=0
+    )
     x_there = np.concatenate([cos, sin], axis=0)
     x_back = np.concatenate([cos, -sin], axis=0)
     upper, edge = order > HALF, (order == 0) | (order == HALF)
@@ -700,22 +702,26 @@
     spread(sums_sent, sums, 0)
 
     slope = jnp.zeros((1, G), F32)
-    for c in range(3):
-        for part in range(PARTS):
-            whole_arrived(c, part).wait()
+    rows_here = G // PARTS
+    for part, c in [(part, c) for part in range(PARTS) for c in range(3)]:
+        whole_arrived(c, part).wait()
+        waves = pl.ds(part * rows_here, rows_here)
 
         def back_step(step, carry):
             stack = []
             for j in range(2):
-                values = arrived[c, pl.ds(2 * step + j, G, stride=8), :]
-                first = back[0] * values + turned(back[1] * values)
-                second = back[2] * values + turned(back[3] * values)
+                values = arrived[c, pl.ds(part * BLOCK + 2 * step + j, rows_here, stride=8), :]
+                first = back[0, waves] * values + turned(back[1, waves] * values)
+                second = back[2, waves] * values + turned(back[3, waves] * values)
                 stack.append(jnp.concatenate([first, second], axis=0))
-            lines = by_left(beside(y_back), jnp.concatenate(stack, axis=1))
+            table = [y_back[n, pl.ds(part * G, G)] for n in range(2)]
+            lines = by_left(table, jnp.concatenate(stack, axis=1))
             cells = by_right(jnp.concatenate([lines[:, :G], lines[:, G:]], axis=0), z_back)
             at = pl.ds(2 * step, 2)
             whole = field[c, at].reshape(2 * G, G) + cells
             field[c, at] = whole.reshape(2, G, G)
+            if part < PARTS - 1:
+                return carry
             return carry - row_sum(whole * tangent[c, at].reshape(2 * G, G))
 
         slope = lax.fori_loop(0, PLANES // 2, back_step, slope)

time: 98.5 us -> 98.4 us (level)
  no operation moved by 1% of the time
where the time goes in v5:
time: 98.4 us; the launch traced here: 98.3 us
  Pallas kernels  97.6 us (99%)
    pallas_call x1, Pallas kernels, local(): pl.pallas_call(kernel, out_shape=(pltpu.VMEM(block, F32), pltpu.VMEM(bloc...  95.8 us

profile of v5, /device:TPU:1, one launch (start us, length us, event | category | flops | bytes accessed | tf_op | source)
XLA Modules:
  0.0 98.3 jit_solution(2625700997626786600)
XLA Ops:
  0.6 0.0 copy-start
  0.6 95.8 %shard_map.140 = (f32[3,8,128,128]{3,2,1,0:T(8,128)S(1)}, f32[3,8,128,128]{3,2,1,0:T(8,128)S(1)}, f32[1,128]{1,0:T(1,128)S(1)}) custom-call(f32[1,3,8,128,128]{4,3,2,1,0:T(8,128)} %moment.1, s32[8,128,128]{2,1,0:T(8,128)} %labels_in.1, f32[6,1024,128]{2,1,0:T(8,128)} %bitcast.1, f32[8]{0:T(128)} %anisotropy_in.1, f32[8]{0:T(128)} %stiffness_in.1, ...), custom_call_target="tpu_custom_call" | custom-call | tf_op jit(solution)/shard_map/pallas_call | solution.py:835
  96.4 0.0 copy-done
  96.4 1.9 %shard_map.141 = (f32[1,3,8,128,128]{4,3,2,1,0:T(8,128)}, f32[1,3,8,128,128]{4,3,2,1,0:T(8,128)}) custom-call(f32[1,3,8,128,128]{4,3,2,1,0:T(8,128)S(1)} %copy-done, f32[3,8,128,128]{3,2,1,0:T(8,128)S(1)} %get-tuple-element.5.normal, f32[3,8,128,128]{3,2,1,0:T(8,128)S(1)} %get-tuple-element.6.tangent, f32[1,128]{1,0:T(1,128)S(1)} %get-tuple-element.7.strength), custom_call_target="tpu_custom_call" | custom-call | tf_op jit(solution)/shard_map/pallas_call | solution.py:889
Async XLA Ops:
  0.6 95.8 %copy-start = (f32[1,3,8,128,128]{4,3,2,1,0:T(8,128)S(1)}, f32[1,3,8,128,128]{4,3,2,1,0:T(8,128)}, u32[]{:S(2)}) copy-start(f32[1,3,8,128,128]{4,3,2,1,0:T(8,128)} %moment.1) | copy-start | bytes 4718596
